TPU v7x, 512 devices: a whole 4x4x16 slice. The times are simulated.
512 devices in a mesh: blk: 32 (over z, x_hi), grp: 16 (over y, x_lo, core).
Axes of the slice: x: 4 (x_hi: 2, x_lo: 2; x = x_hi * 2 + x_lo), y: 4, z: 16, core: 2. Of those that a mesh axis runs over, the one named last changes fastest.
Arguments:
- images: float32 [65536, 1152], P(('blk', 'grp')), may hold values from -6 to 6
- texts: float32 [65536, 1152], P(('blk', 'grp')), may hold values from -6 to 6
- log_scale: float32 [1], replicated, may hold values from 2.3 to 3.4
- bias: float32 [1], replicated, may hold values from -3 to -1
Outputs:
- row_loss: float32 [65536], P(('blk', 'grp'))
- image_grad: float32 [65536, 1152], P(('blk', 'grp'))
- text_grad: float32 [65536, 1152], P(('blk', 'grp'))
All inputs are finite; a program needn't handle non-finite values.
Results may differ from a plain program's by a relative error of at most 0.0056.
Values may be sent and summed in bfloat16 or wider, within the bound.
A program may use at most 64 MiB of HBM per device.

v0:
```python
import jax
import jax.numpy as jnp
from jax import lax
from jax.sharding import PartitionSpec as P

STEPS = 2


def passed_along(x, axis, by):
    size = lax.axis_size(axis)
    return lax.ppermute(x, axis, [(i, (i + by) % size) for i in range(size)])


def prepare(values):
    inverse = lax.rsqrt(jnp.sum(values * values, axis=1, keepdims=True) + 1e-06)
    unit = values * inverse
    return (inverse, unit, unit.astype(jnp.bfloat16))


def backnorm(inverse, unit, grad):
    return inverse * (grad - unit * jnp.sum(unit * grad, axis=1, keepdims=True))


def score_rows(left, right, own_cols, temper, offset, first, want_loss):
    logits = (
        temper * jnp.einsum("rd,cd->rc", left, right, preferred_element_type=jnp.float32) + offset
    )
    if first:
        columns = jnp.arange(right.shape[0], dtype=jnp.int32)
        paired = (own_cols[:, None] == columns[None, :]).astype(jnp.float32)
    else:
        paired = jnp.zeros(logits.shape, jnp.float32)
    weights = (temper * (jax.nn.sigmoid(logits) - paired)).astype(jnp.bfloat16)
    grad = jnp.dot(weights, right, preferred_element_type=jnp.float32)
    if want_loss:
        losses = jnp.where(paired > 0.5, jax.nn.softplus(-logits), jax.nn.softplus(logits))
        return (jnp.sum(losses, axis=1), grad, weights)
    return (None, grad, weights)


def body(images, texts, log_scale, bias):
    rows = images.shape[0]
    width = images.shape[1]
    members = lax.axis_size("grp")
    temper = jnp.exp(log_scale[0])
    offset = bias[0]
    inv_image, image_hat, image_low = prepare(images)
    inv_text, text_hat, text_low = prepare(texts)
    own_cols = lax.axis_index("grp") * rows + jnp.arange(rows, dtype=jnp.int32)
    grad_image = jnp.zeros((rows, width), jnp.float32)
    grad_text = jnp.zeros((rows, width), jnp.float32)
    loss_total = jnp.zeros((rows,), jnp.float32)
    text_block, image_block = (
        lax.all_gather(text_low, "grp", axis=0, tiled=True),
        lax.all_gather(image_low, "grp", axis=0, tiled=True),
    )
    for step in range(STEPS):
        if step > 0:
            text_block = passed_along(text_block, "blk", 1)
            image_block = passed_along(image_block, "blk", -1)
        losses, gimage, weights = score_rows(
            image_low, text_block, own_cols, temper, offset, step == 0, True
        )
        unused, gtext, spare = score_rows(
            text_low, image_block, own_cols, temper, offset, step == 0, False
        )
        loss_total = loss_total + losses
        grad_image = grad_image + gimage
        grad_text = grad_text + gtext
    row_loss = loss_total / (STEPS * rows * members)
    image_grad = backnorm(inv_image, image_hat, grad_image)
    text_grad = backnorm(inv_text, text_hat, grad_text)
    return (row_loss, image_grad, text_grad)


def solution(mesh):
    in_specs = (P(("blk", "grp"), None), P(("blk", "grp"), None), P(), P())
    out_specs = (P(("blk", "grp")), P(("blk", "grp"), None), P(("blk", "grp"), None))
    return jax.shard_map(body, mesh=mesh, in_specs=in_specs, out_specs=out_specs, check_vma=False)
```

profile of v0, /device:TPU:1, one launch (start us, length us, event | category | flops | bytes accessed | tf_op | source)
XLA Modules:
  0.0 322.2 jit_solution(5050286438639307326)
XLA Ops:
  7.2 0.0 all-gather.5.cloned.1.call-start
  7.2 1.2 multiply_reduce_fusion.3
  8.4 1.9 multiply_convert_fusion.3
  10.3 0.0 all-gather.5.cloned.1.call-update
  10.3 0.0 all-gather.3.cloned.1.call-start
  10.4 1.2 multiply_reduce_fusion.2
  11.6 1.9 multiply_convert_fusion.2
  13.4 0.0 all-gather.3.cloned.1.call-update
  13.5 49.2 %all-gather.5.cloned.1.call-done = bf16[2048,1152]{1,0:T(8,128)(2,1)} async-done(((bf16[128,1152]{1,0:T(8,128)(2,1)}), bf16[2048,1152]{1,0:T(8,128)(2,1)}) %all-gather.5.cloned.1.call-update) | async-done | bytes 4718608 | tf_op jit(solution)/shard_map/all_gather | solution.py:55
  62.7 7.8 %collective-permute-start.1 = (bf16[2048,1152]{1,0:T(8,128)(2,1)}, bf16[2048,1152]{1,0:T(8,128)(2,1)}, u32[]{:S(2)}, u32[]{:S(2)}) collective-permute-start(bf16[2048,1152]{1,0:T(8,128)(2,1)} %all-gather.5.cloned.1.call-done), channel_id=1, source_target_pairs={{0,496},{16,0},{32,16},{48,32},{64,48},{80,64},{96,80},{112,96},{1... | collective-permute-start | bytes 14155784 | tf_op jit(solution)/shard_map/ppermute | solution.py:11
  70.5 126.7 %all-gather.3.cloned.1.call-done = bf16[2048,1152]{1,0:T(8,128)(2,1)} async-done(((bf16[128,1152]{1,0:T(8,128)(2,1)}), bf16[2048,1152]{1,0:T(8,128)(2,1)}) %all-gather.3.cloned.1.call-update) | async-done | bytes 4718608 | tf_op jit(solution)/shard_map/all_gather | solution.py:54
  197.2 1.9 collective-permute-start
  200.5 5.0 %fusion.20 = (f32[128]{0:T(128)S(1)}, f32[128,2048]{1,0:T(8,128)S(1)}) fusion(s32[128]{0:T(128)S(1)} %iota_add_fusion, f32[]{:T(128)} %bitcast.14, bf16[128,1152]{1,0:T(8,128)(2,1)} %multiply_convert_fusion.3, bf16[2048,1152]{1,0:T(8,128)(2,1)} %all-gather.3.cloned.1.call-done, f32[]{:T(128)} %bitcast), kind=kOutput, calls=%fused_computation.31 | convolution fusion | flops 609222528 | bytes 6063112 | tf_op jit(solution)/shard_map/rd,cd->rc/dot_general | solution.py:26
  205.5 0.0 copy-start.3
  205.5 1.0 fusion.23
  206.5 0.0 copy-start
  206.5 6.2 %fusion.22 = f32[128,1152]{1,0:T(8,128)S(1)} fusion(bf16[2048,1152]{1,0:T(8,128)(2,1)} %all-gather.5.cloned.1.call-done, bf16[128,1152]{1,0:T(8,128)(2,1)S(1)} %copy-done.3, f32[]{:T(128)} %bitcast.16, f32[]{:T(128)} %bitcast, s32[128]{0:T(128)S(1)} %iota_add_fusion), kind=kOutput, calls=%fused_computation.36 | convolution fusion | flops 1210580992 | bytes 5603848 | tf_op jit(solution)/shard_map/dot_general | solution.py:34
  212.8 6.3 %multiply_reduce_fusion = (f32[128]{0:T(128)S(1)}, f32[128,1152]{1,0:T(8,128)S(1)}) fusion(f32[128,1152]{1,0:T(8,128)S(1)} %copy-done, f32[128]{0:T(128)S(1)} %add_rsqrt_fusion, f32[128,1152]{1,0:T(8,128)S(1)} %fusion.22, bf16[2048,1152]{1,0:T(8,128)(2,1)} %collective-permute-done.1, bf16[128,1152]{1,0:T(8,128)(2,1)S(1)} %copy-done.3, f32[]{:T(128)} %bitcast.15, ...), kind=kOutput, calls=%fused_computation.38 | convolution fusion | flops 1210384256 | bytes 6784008 | tf_op jit(solution)/shard_map/dot_general | solution.py:34
  219.0 1.0 subtract_multiply_fusion
  220.0 86.1 %collective-permute-done = bf16[2048,1152]{1,0:T(8,128)(2,1)} collective-permute-done((bf16[2048,1152]{1,0:T(8,128)(2,1)}, bf16[2048,1152]{1,0:T(8,128)(2,1)}, u32[]{:S(2)}, u32[]{:S(2)}) %collective-permute-start) | collective-permute-done | bytes 4718624 | tf_op jit(solution)/shard_map/ppermute | solution.py:11
  306.1 4.3 %fusion.21 = (f32[128]{0:T(128)S(1)}, f32[128,2048]{1,0:T(8,128)S(1)}) fusion(f32[]{:T(128)} %bitcast.17, bf16[128,1152]{1,0:T(8,128)(2,1)S(1)} %copy-done.2, bf16[2048,1152]{1,0:T(8,128)(2,1)} %collective-permute-done, f32[]{:T(128)} %bitcast), kind=kOutput, calls=%fused_computation.32 | convolution fusion | flops 606338944 | bytes 6062600 | tf_op jit(solution)/shard_map/rd,cd->rc/dot_general | solution.py:26
  310.5 3.4 %multiply_reduce_fusion.1 = (f32[128]{0:T(128)S(1)}, f32[128,1152]{1,0:T(8,128)S(1)}) fusion(f32[128,1152]{1,0:T(8,128)S(1)} %copy-done.1, f32[128]{0:T(128)S(1)} %add_rsqrt_fusion.1, f32[128,1152]{1,0:T(8,128)S(1)} %fusion.23, bf16[2048,1152]{1,0:T(8,128)(2,1)} %collective-permute-done, f32[128,2048]{1,0:T(8,128)S(1)} %get-tuple-element.6, f32[]{:T(128)} %bitcast), kind=kOutput, calls=%fused_computation.40 | convolution fusion | flops 605880192 | bytes 7537668 | tf_op jit(solution)/shard_map/dot_general | solution.py:34
  313.9 1.0 subtract_multiply_fusion.1
  314.9 0.5 add_multiply_fusion
  (12 shorter events, 0.0 us)
Async XLA Ops:
  7.2 55.5 %all-gather.5.cloned.1.call-start = ((), (), s32[]{:S(2)}) async-start(), calls=%async_computation.1 | async-start | bytes 5013504 | tf_op jit(solution)/shard_map/all_gather | solution.py:55
  10.3 186.9 %all-gather.3.cloned.1.call-start = ((), (), s32[]{:S(2)}) async-start(), calls=%async_computation | async-start | bytes 5013504 | tf_op jit(solution)/shard_map/all_gather | solution.py:54
  62.7 150.0 %collective-permute-start.1 = (bf16[2048,1152]{1,0:T(8,128)(2,1)}, bf16[2048,1152]{1,0:T(8,128)(2,1)}, u32[]{:S(2)}, u32[]{:S(2)}) collective-permute-start(bf16[2048,1152]{1,0:T(8,128)(2,1)} %all-gather.5.cloned.1.call-done), channel_id=1, source_target_pairs={{0,496},{16,0},{32,16},{48,32},{64,48},{80,64},{96,80},{112,96},{1... | collective-permute-start | bytes 14155784 | tf_op jit(solution)/shard_map/ppermute | solution.py:11
  197.2 108.9 %collective-permute-start = (bf16[2048,1152]{1,0:T(8,128)(2,1)}, bf16[2048,1152]{1,0:T(8,128)(2,1)}, u32[]{:S(2)}, u32[]{:S(2)}) collective-permute-start(bf16[2048,1152]{1,0:T(8,128)(2,1)} %all-gather.3.cloned.1.call-done), channel_id=1, source_target_pairs={{0,16},{16,32},{32,48},{48,64},{64,80},{80,96},{96,112},{112,128},... | collective-permute-start | bytes 14155784 | tf_op jit(solution)/shard_map/ppermute | solution.py:11
  200.5 5.1 %copy-start.4 = (bf16[2048,1152]{1,0:T(8,128)(2,1)S(1)}, bf16[2048,1152]{1,0:T(8,128)(2,1)}, u32[]{:S(2)}) copy-start(bf16[2048,1152]{1,0:T(8,128)(2,1)} %all-gather.3.cloned.1.call-done) | copy-start | bytes 14155780
  205.5 1.0 copy-start.3
  206.5 6.2 %copy-start = (f32[128,1152]{1,0:T(8,128)S(1)}, f32[128,1152]{1,0:T(8,128)}, u32[]{:S(2)}) copy-start(f32[128,1152]{1,0:T(8,128)} %param.5) | copy-start | bytes 1769476
  212.7 93.4 %copy-start.2 = (bf16[128,1152]{1,0:T(8,128)(2,1)S(1)}, bf16[128,1152]{1,0:T(8,128)(2,1)}, u32[]{:S(2)}) copy-start(bf16[128,1152]{1,0:T(8,128)(2,1)} %multiply_convert_fusion.3) | copy-start | bytes 884740
  219.0 91.4 %copy-start.1 = (f32[128,1152]{1,0:T(8,128)S(1)}, f32[128,1152]{1,0:T(8,128)}, u32[]{:S(2)}) copy-start(f32[128,1152]{1,0:T(8,128)} %param.4) | copy-start | bytes 1769476
Sparse Core Ops, SparseCore 0:
  10.7 51.9 all-gather.4
  65.4 131.7 all-gather.2
where the time goes:
time: 323 us; the launch traced here: 322 us
  waiting for transfers between devices  262 us (81%)
  matrix products  26.2 us (8%)
  between operations  15.5 us (5%)
  starting transfers between devices  9.76 us (3%)
  other arithmetic  8.67 us (3%)
    all_gather x1, waiting for transfers between devices, body(): lax.all_gather(text_low, 'grp', axis=0, tiled=True)  127 us
    ppermute x2, waiting for transfers between devices, passed_along(): return lax.ppermute(x, axis, [(i, (i + by) % size) for i in range(size)])  86.1 us
    all_gather x1, waiting for transfers between devices, body(): lax.all_gather(image_low, 'grp', axis=0, tiled=True)  49.2 us
    dot_general x4, matrix products, score_rows(): grad = jnp.dot(weights, right, preferred_element_type=jnp.float32)  16.9 us
    ppermute x2, starting transfers between devices, passed_along(): return lax.ppermute(x, axis, [(i, (i + by) % size) for i in range(size)])  9.68 us
    dot_general x2, matrix products, score_rows(): jnp.einsum('rd,cd->rc', left, right, preferred_element_type=jnp.float32)  9.37 us
  transfers between devices with their start and end apart: 4, of which 3 were waited for; matrix products, arithmetic and copies ran while one was open for 7% of the time, Pallas kernels for 0%

commit v1 on v0

v1 whole, which is shorter than its diff:
```python
import functools

import jax
import jax.numpy as jnp
from jax import lax
from jax.experimental import pallas as pl
from jax.experimental.pallas import tpu as pltpu
from jax.sharding import PartitionSpec as P

STEPS = 2
MESH = pl.DeviceIdType.MESH
BF = jnp.bfloat16
F32 = jnp.float32

OWN, PAIR, NEAR, FAR = 0, 1, 2, 3
Y_OFF = (0, 1, 3, 2)


def places(n_blk):
    b = lax.axis_index("blk")
    g = lax.axis_index("grp")
    core = lax.rem(g, 2)
    x_lo = lax.rem(g // 2, 2)
    y = g // 4
    nxt = lax.rem(b + 1, n_blk)
    prv = lax.rem(b + n_blk - 1, n_blk)

    def member(yy, xx, kk):
        return (yy * 2 + xx) * 2 + kk

    sibling = (b, member(y, x_lo, 1 - core))
    pair = (b, member(y, 1 - x_lo, core))
    near_to = (nxt, member(y, 1 - x_lo, core))
    far_to = (nxt, member(y, x_lo, core))
    near_of = (prv, member(y, 1 - x_lo, core))
    far_of = (prv, member(y, x_lo, core))
    ring = [(b, member(lax.rem(y + d, 4), x_lo, core)) for d in Y_OFF[1:]]
    return sibling, pair, near_to, far_to, near_of, far_of, ring


def inverse_norm(values):
    return lax.rsqrt(jnp.sum(values * values, axis=1, keepdims=True) + 1e-06)


def kernel(n_blk, mean, ls_ref, bi_ref, img_hbm, txt_hbm, loss_ref, gi_hbm, gt_hbm,
           img, txt, gi, gt, ib, tb, coef, loss, sib_out, sib_in, t_out, t_in, i_out, i_in, l_in,
           lsem, ssem, rsem):
    rows = img.shape[0]
    sibling, pair, near_to, far_to, near_of, far_of, ring = places(n_blk)
    load_t = pltpu.make_async_copy(txt_hbm, txt, lsem.at[0])
    load_i = pltpu.make_async_copy(img_hbm, img, lsem.at[1])
    load_t.start()
    load_i.start()

    barrier = pltpu.get_barrier_semaphore()
    others = [sibling, pair, near_to, far_to, near_of, far_of] + ring
    for other in others:
        pl.semaphore_signal(barrier, inc=1, device_id=other, device_id_type=MESH)

    count = iter(range(64))

    def send(src, dst, to):
        s = next(count)
        return pltpu.make_async_remote_copy(
            src_ref=src, dst_ref=dst, send_sem=ssem.at[s], recv_sem=rsem.at[s],
            device_id=to, device_id_type=MESH)

    load_t.wait()
    inv_t = inverse_norm(txt[...])
    tb[0, 0] = (txt[...] * inv_t).astype(BF)
    load_i.wait()
    inv_i = inverse_norm(img[...])
    ib[0] = (img[...] * inv_i).astype(BF)
    pl.semaphore_wait(barrier, len(others))

    t_copies = [send(tb.at[0, 0], tb.at[s, 0], to)
                for s, to in ((PAIR, pair), (NEAR, near_to), (FAR, far_to))]
    i_copies = [send(ib.at[0], ib.at[slot], ring[j]) for j, slot in ((0, 2), (1, 1), (2, 3))]
    s_copies = [send(tb.at[s, 0], tb.at[s, 1], sibling) for s in range(4)]
    for c in (t_copies[0], i_copies[0], t_copies[1], i_copies[1], t_copies[2], i_copies[2], s_copies[0]):
        c.start()

    temper = jnp.exp(jnp.full((1, rows), ls_ref[0], F32))
    offset = bi_ref[0]
    loss[...] = jnp.zeros_like(loss)

    def score(s, lo, hi):
        left = tb[s].reshape(2 * rows, tb.shape[-1])
        for slot in range(lo, hi):
            logit = lax.dot_general(left, ib[slot], (((1,), (1,)), ((), ())), preferred_element_type=F32)
            logit = temper * logit + offset
            e = jnp.exp(-jnp.abs(logit))
            r = 1.0 / (1.0 + e)
            weight = jnp.where(logit >= 0, r, e * r)
            signed = logit
            if s == OWN and slot == 0:
                paired = (lax.broadcasted_iota(jnp.int32, logit.shape, 0)
                          == lax.broadcasted_iota(jnp.int32, logit.shape, 1))
                weight = weight - paired.astype(F32)
                signed = jnp.where(paired, -logit, logit)
            lost = jnp.maximum(signed, 0.0) + jnp.where(e < 1e-3, e * (1.0 - 0.5 * e), jnp.log(1.0 + e))
            loss[slot] += jnp.sum(lost.reshape(2 * rows // 8, 8, rows), axis=0)
            coef[pl.ds(s * 2 * rows, 2 * rows), pl.ds(slot * rows, rows)] = (temper * weight).astype(BF)

    def text_partial(s):
        return jnp.dot(coef[pl.ds(s * 2 * rows, 2 * rows), :], ib[...].reshape(4 * rows, ib.shape[-1]),
                       preferred_element_type=F32)

    def image_partial(slot):
        return lax.dot_general(coef[:, pl.ds(slot * rows, rows)], tb[...].reshape(8 * rows, tb.shape[-1]),
                               (((0,), (0,)), ((), ())), preferred_element_type=F32)

    s_copies[0].wait_recv()
    score(OWN, 0, 1)
    t_copies[0].wait_recv()
    s_copies[1].start()
    t_copies[1].wait_recv()
    s_copies[2].start()
    i_copies[0].wait_recv()
    i_copies[1].wait_recv()
    score(OWN, 1, 3)
    s_copies[1].wait_recv()
    score(PAIR, 0, 3)
    s_copies[2].wait_recv()
    score(NEAR, 0, 3)
    t_copies[2].wait_recv()
    s_copies[3].start()
    i_copies[2].wait_recv()
    for s in (PAIR, NEAR, OWN):
        score(s, 3, 4)

    back = [send(sib_out.at[s], sib_in.at[s], sibling) for s in range(4)]
    t_back = [None] + [send(t_out.at[s - 1], t_in.at[s - 1], to)
                       for s, to in ((PAIR, pair), (NEAR, near_of), (FAR, far_of))]
    i_back = [None] + [send(i_out.at[j], i_in.at[(1, 0, 2)[j]], ring[j]) for j in range(3)]
    l_back = [None] + [send(loss.at[j + 1], l_in.at[(1, 0, 2)[j]], ring[j]) for j in range(3)]
    held = {}

    def start_text(s):
        part = text_partial(s)
        sib_out[s] = part[rows:].astype(BF)
        back[s].start()
        held[s] = part[:rows]

    def finish_text(s):
        back[s].wait_recv()
        whole = held[s] + sib_in[s].astype(F32)
        if s == OWN:
            gt[...] = whole
        else:
            t_out[s - 1] = whole.astype(BF)
            t_back[s].start()

    start_text(PAIR)
    start_text(NEAR)
    s_copies[3].wait_recv()
    score(FAR, 0, 4)
    finish_text(PAIR)
    finish_text(NEAR)
    start_text(FAR)
    for slot in (3, 1, 2):
        i_out[slot - 1] = image_partial(slot).astype(BF)
        i_back[slot].start()
        l_back[slot].start()
        if slot == 3:
            finish_text(FAR)
    gi[...] = image_partial(0)
    start_text(OWN)
    finish_text(OWN)

    def backnorm(values, inverse, grad):
        unit = values * inverse
        return inverse * (grad - unit * jnp.sum(unit * grad, axis=1, keepdims=True))

    for c in l_back[1:]:
        c.wait_recv()
    total = loss[0] + l_in[0] + l_in[1] + l_in[2]
    loss_ref[...] = jnp.sum(total, axis=0, keepdims=True) / mean

    for c in i_back[1:]:
        c.wait_recv()
    grad = gi[...] + i_in[0].astype(F32) + i_in[1].astype(F32) + i_in[2].astype(F32)
    gi[...] = backnorm(img[...], inv_i, grad)
    put_i = pltpu.make_async_copy(gi, gi_hbm, lsem.at[0])
    put_i.start()
    for c in t_back[1:]:
        c.wait_recv()
    grad = gt[...] + t_in[0].astype(F32) + t_in[1].astype(F32) + t_in[2].astype(F32)
    gt[...] = backnorm(txt[...], inv_t, grad)
    put_t = pltpu.make_async_copy(gt, gt_hbm, lsem.at[1])
    put_t.start()
    for c in t_copies + i_copies + s_copies + back + t_back[1:] + i_back[1:] + l_back[1:]:
        c.wait_send()
    put_i.wait()
    put_t.wait()


def body(images, texts, log_scale, bias):
    rows, width = images.shape
    n_blk = lax.axis_size("blk")
    mean = STEPS * rows * lax.axis_size("grp")
    half = functools.partial(pltpu.VMEM, dtype=BF)
    full = functools.partial(pltpu.VMEM, dtype=F32)
    any_space = pl.BlockSpec(memory_space=pl.ANY)
    row_loss, image_grad, text_grad = pl.pallas_call(
        functools.partial(kernel, n_blk, mean),
        out_shape=(
            jax.ShapeDtypeStruct((1, rows), F32),
            jax.ShapeDtypeStruct((rows, width), F32),
            jax.ShapeDtypeStruct((rows, width), F32),
        ),
        in_specs=[pl.BlockSpec(memory_space=pltpu.SMEM)] * 2 + [any_space] * 2,
        out_specs=(pl.BlockSpec(memory_space=pltpu.VMEM), any_space, any_space),
        scratch_shapes=[
            full((rows, width)), full((rows, width)), full((rows, width)), full((rows, width)),
            half((4, rows, width)),
            half((4, 2, rows, width)),
            half((8 * rows, 4 * rows)),
            full((4, 8, rows)),
            half((4, rows, width)), half((4, rows, width)),
            half((3, rows, width)), half((3, rows, width)),
            half((3, rows, width)), half((3, rows, width)),
            full((3, 8, rows)),
            pltpu.SemaphoreType.DMA((2,)),
            pltpu.SemaphoreType.DMA((23,)),
            pltpu.SemaphoreType.DMA((23,)),
        ],
        compiler_params=pltpu.CompilerParams(
            collective_id=0, has_side_effects=True, vmem_limit_bytes=40 << 20),
        name="pair_loss",
    )(log_scale, bias, images, texts)
    return row_loss.reshape(rows), image_grad, text_grad


def solution(mesh):
    in_specs = (P(("blk", "grp"), None), P(("blk", "grp"), None), P(), P())
    out_specs = (P(("blk", "grp")), P(("blk", "grp"), None), P(("blk", "grp"), None))
    return jax.shard_map(body, mesh=mesh, in_specs=in_specs, out_specs=out_specs, check_vma=False)
```

time: 323 us -> 57.6 us (0.18)
  waiting for transfers between devices: 262 us -> 0 us
  Pallas kernels: 0 us -> 51.2 us
  matrix products: 26.2 us -> 0 us
  between operations: 15.5 us -> 1.94 us
  starting transfers between devices: 9.76 us -> 0 us
  other arithmetic: 8.67 us -> 0 us
  local copies, waits for them, and re-layouts: 0.03 us -> 4.26 us
    all_gather x2 -> x0, waiting for transfers between devices: 176 us -> none  [the longest x1 127 us: body(): lax.all_gather(text_low, 'grp', axis=0, tiled=True)]
    ppermute x2 -> x0, waiting for transfers between devices: 86.1 us -> none  [passed_along(): return lax.ppermute(x, axis, [(i, (i + by) % size) for i in range(size)])]
    pallas_call x0 -> x1, Pallas kernels: none -> 51.2 us  [body(): pl.pallas_call(functools.partial(kernel, n_blk, mean), out_shape=(jax.Sha...]
    dot_general x6 -> x0, matrix products: 26.2 us -> none  [the longest x4 16.9 us: score_rows(): grad = jnp.dot(weights, right, preferred_element_type=jnp.float32)]
    ppermute x2 -> x0, starting transfers between devices: 9.68 us -> none  [passed_along(): return lax.ppermute(x, axis, [(i, (i + by) % size) for i in range(size)])]
    unnamed x10 -> x7, local copies, waits for them, and re-layouts: 0.03 us -> 4.26 us
    convert_element_type x2 -> x0, other arithmetic: 3.77 us -> none  [prepare(): return (inverse, unit, unit.astype(jnp.bfloat16))]
  transfers between devices with their start and end apart: 4 -> 0, of which waited for: 3 -> 0; matrix products, arithmetic and copies ran while one was open for 7% -> 0% of each run, Pallas kernels for 0% -> 0%
where the time goes in v1:
time: 57.6 us; the launch traced here: 57.4 us
  Pallas kernels  51.2 us (89%)
  local copies, waits for them, and re-layouts  4.26 us (7%)
  between operations  1.94 us (3%)
    pallas_call x1, Pallas kernels, body(): pl.pallas_call(functools.partial(kernel, n_blk, mean), out_shape=(jax.Sha...  51.2 us
    unnamed x7, local copies, waits for them, and re-layouts  4.26 us

profile of v1, /device:TPU:1, one launch (start us, length us, event | category | flops | bytes accessed | tf_op | source)
XLA Modules:
  0.0 57.4 jit_solution(9398876756014786797)
XLA Ops:
  1.9 0.0 copy-start
  1.9 1.1 %copy-done = f32[128,1152]{1,0:T(8,128)S(1)} copy-done((f32[128,1152]{1,0:T(8,128)S(1)}, f32[128,1152]{1,0:T(8,128)}, u32[]{:S(2)}) %copy-start) | copy-done | bytes 589848
  3.0 0.0 copy-start.1
  3.0 1.1 %copy-done.1 = f32[128,1152]{1,0:T(8,128)S(1)} copy-done((f32[128,1152]{1,0:T(8,128)S(1)}, f32[128,1152]{1,0:T(8,128)}, u32[]{:S(2)}) %copy-start.1) | copy-done | bytes 589848
  4.1 51.2 %pair_loss.1 = (f32[1,128]{1,0:T(1,128)S(1)}, f32[128,1152]{1,0:T(8,128)S(1)}, f32[128,1152]{1,0:T(8,128)S(1)}) custom-call(f32[1]{0:T(128)S(6)} %copy.10.ls_ref, f32[1]{0:T(128)S(6)} %copy.11.bi_ref, f32[128,1152]{1,0:T(8,128)S(1)} %copy-done, f32[128,1152]{1,0:T(8,128)S(1)} %copy-done.1), custom_call_target="tpu_custom_call" | custom-call | tf_op jit(solution)/shard_map/pair_loss/pallas_call | solution.py:205
  55.2 0.5 copy.12
  55.8 0.8 %copy.13 = f32[128,1152]{1,0:T(8,128)} copy(f32[128,1152]{1,0:T(8,128)S(1)} %get-tuple-element.13) | data formatting | bytes 1179648
  56.6 0.8 %copy.14 = f32[128,1152]{1,0:T(8,128)} copy(f32[128,1152]{1,0:T(8,128)S(1)} %get-tuple-element.14) | data formatting | bytes 1179648
Async XLA Ops:
  1.9 1.1 %copy-start = (f32[128,1152]{1,0:T(8,128)S(1)}, f32[128,1152]{1,0:T(8,128)}, u32[]{:S(2)}) copy-start(f32[128,1152]{1,0:T(8,128)} %img_hbm.1) | copy-start | bytes 1769476
  3.0 1.1 %copy-start.1 = (f32[128,1152]{1,0:T(8,128)S(1)}, f32[128,1152]{1,0:T(8,128)}, u32[]{:S(2)}) copy-start(f32[128,1152]{1,0:T(8,128)} %txt_hbm.1) | copy-start | bytes 1769476

commit v2 on v1

v2 whole, which is shorter than its diff:
```python
import functools

import jax
import jax.numpy as jnp
from jax import lax
from jax.experimental import pallas as pl
from jax.experimental.pallas import tpu as pltpu
from jax.sharding import PartitionSpec as P

STEPS = 2
MESH = pl.DeviceIdType.MESH
BF = jnp.bfloat16
F32 = jnp.float32
N_SEMS = 36

OWN, PAIR, NEAR, FAR = 0, 1, 2, 3
RIGHT, LEFT, OPP = 1, 2, 3


def places(n_blk):
    b = lax.axis_index("blk")
    g = lax.axis_index("grp")
    core = lax.rem(g, 2)
    x_lo = lax.rem(g // 2, 2)
    y = g // 4
    nxt = lax.rem(b + 1, n_blk)
    prv = lax.rem(b + n_blk - 1, n_blk)

    def member(yy, xx, kk):
        return (yy * 2 + xx) * 2 + kk

    sibling = (b, member(y, x_lo, 1 - core))
    pair = (b, member(y, 1 - x_lo, core))
    near_to = (nxt, member(y, 1 - x_lo, core))
    near_of = (prv, member(y, 1 - x_lo, core))
    right = (b, member(lax.rem(y + 1, 4), x_lo, core))
    left = (b, member(lax.rem(y + 3, 4), x_lo, core))
    return sibling, pair, near_to, near_of, right, left


def inverse_norm(values):
    return lax.rsqrt(jnp.sum(values * values, axis=1, keepdims=True) + 1e-06)


def kernel(n_blk, mean, ls_ref, bi_ref, img_hbm, txt_hbm, loss_ref, gi_hbm, gt_hbm,
           img, txt, gi, gt, ib, tb, coef, loss, sib_out, sib_in,
           t_out, t_mid, t_in, i_out, i_mid, i_in, l_mid, l_in, lsem, ssem, rsem):
    rows, width = img.shape
    half = rows // 2
    h0, h1 = pl.ds(0, half), pl.ds(half, half)
    sibling, pair, near_to, near_of, right, left = places(n_blk)
    load_t = pltpu.make_async_copy(txt_hbm, txt, lsem.at[0])
    load_i = pltpu.make_async_copy(img_hbm, img, lsem.at[1])
    load_t.start()
    load_i.start()

    barrier = pltpu.get_barrier_semaphore()
    others = [sibling, pair, near_to, near_of, right, left]
    for other in others:
        pl.semaphore_signal(barrier, inc=1, device_id=other, device_id_type=MESH)

    sent = []

    def copy_to(src, dst, to):
        s = len(sent)
        copy = pltpu.make_async_remote_copy(
            src_ref=src, dst_ref=dst, send_sem=ssem.at[s], recv_sem=rsem.at[s],
            device_id=to, device_id_type=MESH)
        sent.append(copy)
        return copy

    def arrived(name, *copies):
        with jax.named_scope("wait_" + name):
            for c in copies:
                c.wait_recv()

    with jax.named_scope("normalize"):
        load_t.wait()
        inv_t = inverse_norm(txt[...])
        tb[OWN, 0] = (txt[...] * inv_t).astype(BF)
        load_i.wait()
        inv_i = inverse_norm(img[...])
        ib[0] = (img[...] * inv_i).astype(BF)
    with jax.named_scope("barrier"):
        pl.semaphore_wait(barrier, len(others))

    t_p0 = copy_to(tb.at[OWN, 0, h0], tb.at[PAIR, 0, h0], pair)
    t_n1 = copy_to(tb.at[OWN, 0, h1], tb.at[NEAR, 0, h1], near_to)
    i_r0 = copy_to(ib.at[0, h0], ib.at[LEFT, h0], right)
    i_l1 = copy_to(ib.at[0, h1], ib.at[RIGHT, h1], left)
    t_p1 = copy_to(tb.at[OWN, 0, h1], tb.at[PAIR, 0, h1], pair)
    t_n0 = copy_to(tb.at[OWN, 0, h0], tb.at[NEAR, 0, h0], near_to)
    i_r1 = copy_to(ib.at[0, h1], ib.at[LEFT, h1], right)
    i_l0 = copy_to(ib.at[0, h0], ib.at[RIGHT, h0], left)
    s_own = copy_to(tb.at[OWN, 0], tb.at[OWN, 1], sibling)
    for c in sent:
        c.start()
    t_f0 = copy_to(tb.at[PAIR, 0, h0], tb.at[FAR, 0, h0], near_to)
    t_f1 = copy_to(tb.at[NEAR, 0, h1], tb.at[FAR, 0, h1], pair)
    i_o0 = copy_to(ib.at[LEFT, h0], ib.at[OPP, h0], right)
    i_o1 = copy_to(ib.at[RIGHT, h1], ib.at[OPP, h1], left)
    s_pair = copy_to(tb.at[PAIR, 0], tb.at[PAIR, 1], sibling)
    s_near = copy_to(tb.at[NEAR, 0], tb.at[NEAR, 1], sibling)
    s_f0 = copy_to(tb.at[FAR, 0, h0], tb.at[FAR, 1, h0], sibling)
    s_f1 = copy_to(tb.at[FAR, 0, h1], tb.at[FAR, 1, h1], sibling)

    temper = jnp.exp(jnp.full((1, rows), ls_ref[0], F32))
    offset = bi_ref[0]
    loss[...] = jnp.zeros_like(loss)

    def score(s, lo, hi):
        with jax.named_scope(f"score_{s}_{lo}_{hi}"):
            chunk = tb[s].reshape(2 * rows, width)
            for slot in range(lo, hi):
                logit = lax.dot_general(chunk, ib[slot], (((1,), (1,)), ((), ())), preferred_element_type=F32)
                logit = temper * logit + offset
                e = jnp.exp(-jnp.abs(logit))
                v = 1.0 + e
                r = 1.0 / v
                weight = jnp.where(logit >= 0, r, e * r)
                signed = logit
                if s == OWN and slot == 0:
                    paired = (lax.broadcasted_iota(jnp.int32, logit.shape, 0)
                              == lax.broadcasted_iota(jnp.int32, logit.shape, 1))
                    weight = weight - paired.astype(F32)
                    signed = jnp.where(paired, -logit, logit)
                lost = jnp.maximum(signed, 0.0) + jnp.where(e < 1e-3, e * (1.0 - 0.5 * e), jnp.log(v))
                loss[slot] += jnp.sum(lost.reshape(2 * rows // 8, 8, rows), axis=0)
                coef[pl.ds(s * 2 * rows, 2 * rows), pl.ds(slot * rows, rows)] = (temper * weight).astype(BF)

    def image_partial(slot):
        return lax.dot_general(coef[:, pl.ds(slot * rows, rows)], tb[...].reshape(8 * rows, width),
                               (((0,), (0,)), ((), ())), preferred_element_type=F32)

    arrived("own_sibling", s_own)
    score(OWN, 0, 1)
    arrived("first_t", t_p0, t_n1)
    t_f0.start()
    t_f1.start()
    arrived("first_i", i_r0, i_l1)
    i_o0.start()
    i_o1.start()
    arrived("second_p", t_p1)
    s_pair.start()
    arrived("second_n", t_n0)
    s_near.start()
    arrived("second_i", i_r1, i_l0)
    score(OWN, 1, 3)
    arrived("pair_sibling", s_pair)
    score(PAIR, 0, 3)
    arrived("near_sibling", s_near)
    score(NEAR, 0, 3)
    arrived("far_t0", t_f0)
    s_f0.start()
    arrived("far_t1", t_f1)
    s_f1.start()
    arrived("opp_i", i_o0, i_o1)
    for s in (PAIR, NEAR, OWN):
        score(s, OPP, OPP + 1)
    arrived("far_sibling", s_f0, s_f1)
    score(FAR, 0, 4)

    back = [copy_to(sib_out.at[s], sib_in.at[s], sibling) for s in range(4)]
    held = {}

    def start_text(s):
        with jax.named_scope(f"text_{s}"):
            part = jnp.dot(coef[pl.ds(s * 2 * rows, 2 * rows), :], ib[...].reshape(4 * rows, width),
                           preferred_element_type=F32)
            sib_out[s] = part[rows:].astype(BF)
            back[s].start()
            held[s] = part[:rows]

    def finish_text(s):
        arrived(f"text_sibling_{s}", back[s])
        whole = held[s] + sib_in[s].astype(F32)
        if s == OWN:
            gt[...] = whole
        else:
            t_out[s - 1] = whole.astype(BF)

    def image(slot):
        with jax.named_scope(f"image_{slot}"):
            i_out[slot - 1] = image_partial(slot).astype(BF)

    f_p0 = copy_to(t_out.at[FAR - 1, h0], t_mid.at[0], pair)
    f_n1 = copy_to(t_out.at[FAR - 1, h1], t_mid.at[1], near_of)
    b_p0 = copy_to(t_out.at[PAIR - 1, h0], t_in.at[0, h0], pair)
    b_p1 = copy_to(t_out.at[PAIR - 1, h1], t_in.at[0, h1], pair)
    b_n1 = copy_to(t_out.at[NEAR - 1, h1], t_in.at[1, h1], near_of)
    b_n0 = copy_to(t_out.at[NEAR - 1, h0], t_in.at[1, h0], near_of)
    f_r0 = copy_to(i_out.at[OPP - 1, h0], i_mid.at[0], right)
    f_l1 = copy_to(i_out.at[OPP - 1, h1], i_mid.at[1], left)
    b_r1 = copy_to(i_out.at[RIGHT - 1, h1], i_in.at[0, h1], right)
    b_r0 = copy_to(i_out.at[RIGHT - 1, h0], i_in.at[0, h0], right)
    b_l0 = copy_to(i_out.at[LEFT - 1, h0], i_in.at[1, h0], left)
    b_l1 = copy_to(i_out.at[LEFT - 1, h1], i_in.at[1, h1], left)
    l_o = copy_to(loss.at[OPP], l_mid, right)
    l_r = copy_to(loss.at[RIGHT], l_in.at[0], right)
    l_l = copy_to(loss.at[LEFT], l_in.at[1], left)

    l_o.start()
    start_text(FAR)
    image(OPP)
    f_r0.start()
    f_l1.start()
    l_l.start()
    finish_text(FAR)
    f_p0.start()
    f_n1.start()
    image(RIGHT)
    b_r1.start()
    image(LEFT)
    b_l0.start()
    start_text(PAIR)
    start_text(NEAR)
    finish_text(PAIR)
    b_p0.start()
    finish_text(NEAR)
    b_n1.start()
    start_text(OWN)
    with jax.named_scope("image_0"):
        gi[...] = image_partial(0)

    def pass_on(name, got, src, slot, part, out):
        arrived(name, got)
        src[slot, part] = (src[slot, part].astype(F32) + out[0][out[1]].astype(F32)).astype(BF)

    arrived("mid_loss", l_o)
    loss[RIGHT] += l_mid[...]
    l_r.start()
    pass_on("mid_r", f_r0, i_out, RIGHT - 1, h0, (i_mid, 0))
    b_r0.start()
    pass_on("mid_l", f_l1, i_out, LEFT - 1, h1, (i_mid, 1))
    b_l1.start()
    pass_on("mid_n", f_p0, t_out, NEAR - 1, h0, (t_mid, 0))
    b_n0.start()
    pass_on("mid_p", f_n1, t_out, PAIR - 1, h1, (t_mid, 1))
    b_p1.start()
    finish_text(OWN)

    def backnorm(values, inverse, grad):
        unit = values * inverse
        return inverse * (grad - unit * jnp.sum(unit * grad, axis=1, keepdims=True))

    arrived("loss", l_r, l_l)
    total = loss[0] + l_in[0] + l_in[1]
    loss_ref[...] = jnp.sum(total, axis=0, keepdims=True) / mean

    arrived("image_back", b_r1, b_l0, b_r0, b_l1)
    grad = gi[...] + i_in[0].astype(F32) + i_in[1].astype(F32)
    gi[...] = backnorm(img[...], inv_i, grad)
    put_i = pltpu.make_async_copy(gi, gi_hbm, lsem.at[0])
    put_i.start()
    arrived("text_back", b_p0, b_n1, b_n0, b_p1)
    grad = gt[...] + t_in[0].astype(F32) + t_in[1].astype(F32)
    gt[...] = backnorm(txt[...], inv_t, grad)
    put_t = pltpu.make_async_copy(gt, gt_hbm, lsem.at[1])
    put_t.start()
    with jax.named_scope("sends_end"):
        for c in sent:
            c.wait_send()
    with jax.named_scope("put"):
        put_i.wait()
        put_t.wait()


def body(images, texts, log_scale, bias):
    rows, width = images.shape
    n_blk = lax.axis_size("blk")
    mean = STEPS * rows * lax.axis_size("grp")
    low = functools.partial(pltpu.VMEM, dtype=BF)
    full = functools.partial(pltpu.VMEM, dtype=F32)
    any_space = pl.BlockSpec(memory_space=pl.ANY)
    row_loss, image_grad, text_grad = pl.pallas_call(
        functools.partial(kernel, n_blk, mean),
        out_shape=(
            jax.ShapeDtypeStruct((1, rows), F32),
            jax.ShapeDtypeStruct((rows, width), F32),
            jax.ShapeDtypeStruct((rows, width), F32),
        ),
        in_specs=[pl.BlockSpec(memory_space=pltpu.SMEM)] * 2 + [any_space] * 2,
        out_specs=(pl.BlockSpec(memory_space=pltpu.VMEM), any_space, any_space),
        scratch_shapes=[
            full((rows, width)), full((rows, width)), full((rows, width)), full((rows, width)),
            low((4, rows, width)),
            low((4, 2, rows, width)),
            low((8 * rows, 4 * rows)),
            full((4, 8, rows)),
            low((4, rows, width)), low((4, rows, width)),
            low((3, rows, width)), low((2, rows // 2, width)), low((2, rows, width)),
            low((3, rows, width)), low((2, rows // 2, width)), low((2, rows, width)),
            full((8, rows)), full((2, 8, rows)),
            pltpu.SemaphoreType.DMA((2,)),
            pltpu.SemaphoreType.DMA((N_SEMS,)),
            pltpu.SemaphoreType.DMA((N_SEMS,)),
        ],
        compiler_params=pltpu.CompilerParams(
            collective_id=0, has_side_effects=True, vmem_limit_bytes=62 << 20),
        name="pair_loss",
    )(log_scale, bias, images, texts)
    return row_loss.reshape(rows), image_grad, text_grad


def solution(mesh):
    in_specs = (P(("blk", "grp"), None), P(("blk", "grp"), None), P(), P())
    out_specs = (P(("blk", "grp")), P(("blk", "grp"), None), P(("blk", "grp"), None))
    return jax.shard_map(body, mesh=mesh, in_specs=in_specs, out_specs=out_specs, check_vma=False)
```

time: 57.6 us -> 50.9 us (0.88)
  Pallas kernels: 51.2 us -> 44.9 us
    pallas_call x1, Pallas kernels: 51.2 us -> 44.9 us  [body(): pl.pallas_call(functools.partial(kernel, n_blk, mean), out_shape=(jax.Sha...]
where the time goes in v2:
time: 50.9 us; the launch traced here: 50.8 us
  Pallas kernels  44.9 us (88%)
  local copies, waits for them, and re-layouts  3.92 us (8%)
  between operations  1.94 us (4%)
    pallas_call x1, Pallas kernels, body(): pl.pallas_call(functools.partial(kernel, n_blk, mean), out_shape=(jax.Sha...  44.9 us
    unnamed x7, local copies, waits for them, and re-layouts  3.92 us

profile of v2, /device:TPU:1, one launch (start us, length us, event | category | flops | bytes accessed | tf_op | source)
XLA Modules:
  0.0 50.8 jit_solution(9578481576974442127)
XLA Ops:
  1.9 44.9 %pair_loss.1 = (f32[1,128]{1,0:T(1,128)}, f32[128,1152]{1,0:T(8,128)}, f32[128,1152]{1,0:T(8,128)}) custom-call(f32[1]{0:T(128)S(6)} %copy.10.ls_ref, f32[1]{0:T(128)S(6)} %copy.11.bi_ref, f32[128,1152]{1,0:T(8,128)} %img_hbm.1, f32[128,1152]{1,0:T(8,128)} %txt_hbm.1), custom_call_target="tpu_custom_call" | custom-call | tf_op jit(solution)/shard_map/pair_loss/pallas_call | solution.py:275
  46.8 0.0 copy-start.1
  46.8 0.6 %copy-done.1 = f32[1,128]{1,0:T(1,128)S(1)} copy-done((f32[1,128]{1,0:T(1,128)S(1)}, f32[1,128]{1,0:T(1,128)}, u32[]{:S(2)}) %copy-start.1) | copy-done | bytes 536
  47.4 0.5 %copy.12 = f32[128]{0:T(128)} copy(f32[128]{0:T(128)S(1)} %bitcast.1) | data formatting | bytes 1024
  48.0 0.0 copy-start
  48.0 2.0 %copy.13 = f32[128,1152]{1,0:T(8,128)} copy(f32[128,1152]{1,0:T(8,128)} %get-tuple-element.13) | data formatting | bytes 1179648
  49.9 0.0 copy-done
  49.9 0.8 %copy.14 = f32[128,1152]{1,0:T(8,128)} copy(f32[128,1152]{1,0:T(8,128)S(1)} %copy-done) | data formatting | bytes 1179648
Async XLA Ops:
  46.8 0.6 %copy-start.1 = (f32[1,128]{1,0:T(1,128)S(1)}, f32[1,128]{1,0:T(1,128)}, u32[]{:S(2)}) copy-start(f32[1,128]{1,0:T(1,128)} %get-tuple-element.6) | copy-start | bytes 1540
  48.0 2.0 %copy-start = (f32[128,1152]{1,0:T(8,128)S(1)}, f32[128,1152]{1,0:T(8,128)}, u32[]{:S(2)}) copy-start(f32[128,1152]{1,0:T(8,128)} %get-tuple-element.14) | copy-start | bytes 1769476

commit v3 on v2

v3 whole, which is shorter than its diff:
```python
import functools

import jax
import jax.numpy as jnp
from jax import lax
from jax.experimental import pallas as pl
from jax.experimental.pallas import tpu as pltpu
from jax.sharding import PartitionSpec as P

STEPS = 2
MESH = pl.DeviceIdType.MESH
BF = jnp.bfloat16
F32 = jnp.float32
N_SEMS = 38
GROUP = 16
PARTS = 4

OWN, PAIR, NEAR, FAR = 0, 1, 2, 3
RIGHT, LEFT, OPP = 1, 2, 3


def places(n_blk):
    b = lax.axis_index("blk")
    g = lax.axis_index("grp")
    core = lax.rem(g, 2)
    x_lo = lax.rem(g // 2, 2)
    y = g // 4
    nxt = lax.rem(b + 1, n_blk)
    prv = lax.rem(b + n_blk - 1, n_blk)

    def member(yy, xx, kk):
        return (yy * 2 + xx) * 2 + kk

    sibling = (b, member(y, x_lo, 1 - core))
    pair = (b, member(y, 1 - x_lo, core))
    near_to = (nxt, member(y, 1 - x_lo, core))
    near_of = (prv, member(y, 1 - x_lo, core))
    right = (b, member(lax.rem(y + 1, 4), x_lo, core))
    left = (b, member(lax.rem(y + 3, 4), x_lo, core))
    return sibling, pair, near_to, near_of, right, left


def inverse_norm(values):
    return lax.rsqrt(jnp.sum(values * values, axis=1, keepdims=True) + 1e-06)


def kernel(n_blk, mean, ls_hbm, bi_hbm, img_hbm, txt_hbm, loss_hbm, gi_hbm, gt_hbm,
           ls_ref, bi_ref, img, txt, gi, gt, row, ib, tb, tf, coef, coef_f, loss, sib_out, sib_in,
           t_out, t_mid, t_in, i_out, i_mid, i_in, l_mid, l_in, lsem, ssem, rsem):
    rows, width = img.shape
    half = rows // 2
    h0, h1 = pl.ds(0, half), pl.ds(half, half)
    sibling, pair, near_to, near_of, right, left = places(n_blk)
    load_t = pltpu.make_async_copy(txt_hbm, txt, lsem.at[0])
    load_i = pltpu.make_async_copy(img_hbm, img, lsem.at[1])
    load_t.start()
    load_i.start()
    load_s = pltpu.make_async_copy(ls_hbm, ls_ref, lsem.at[2])
    load_b = pltpu.make_async_copy(bi_hbm, bi_ref, lsem.at[3])
    load_s.start()
    load_b.start()

    barrier = pltpu.get_barrier_semaphore()
    others = [sibling, pair, near_of, right, left]
    for other in others:
        pl.semaphore_signal(barrier, inc=1, device_id=other, device_id_type=MESH)

    sent = []

    def copy_to(src, dst, to):
        s = len(sent)
        copy = pltpu.make_async_remote_copy(
            src_ref=src, dst_ref=dst, send_sem=ssem.at[s], recv_sem=rsem.at[s],
            device_id=to, device_id_type=MESH)
        sent.append(copy)
        return copy

    def arrived(name, *copies):
        with jax.named_scope("wait_" + name):
            for c in copies:
                c.wait_recv()

    with jax.named_scope("normalize"):
        load_t.wait()
        inv_t = inverse_norm(txt[...])
        tb[0, OWN] = (txt[...] * inv_t).astype(BF)
        load_i.wait()
        inv_i = inverse_norm(img[...])
        ib[0] = (img[...] * inv_i).astype(BF)
    with jax.named_scope("barrier"):
        pl.semaphore_wait(barrier, len(others))

    t_p0 = copy_to(tb.at[0, OWN, h0], tb.at[0, PAIR, h0], pair)
    t_n1 = copy_to(tb.at[0, OWN, h1], tb.at[0, NEAR, h1], near_to)
    i_r0 = copy_to(ib.at[0, h0], ib.at[LEFT, h0], right)
    i_l1 = copy_to(ib.at[0, h1], ib.at[RIGHT, h1], left)
    t_p1 = copy_to(tb.at[0, OWN, h1], tb.at[0, PAIR, h1], pair)
    t_n0 = copy_to(tb.at[0, OWN, h0], tb.at[0, NEAR, h0], near_to)
    i_r1 = copy_to(ib.at[0, h1], ib.at[LEFT, h1], right)
    i_l0 = copy_to(ib.at[0, h0], ib.at[RIGHT, h0], left)
    s_own = copy_to(tb.at[0, OWN], tb.at[1, OWN], sibling)
    for c in sent:
        c.start()
    t_f0 = copy_to(tb.at[0, PAIR, h0], tf.at[0, h0], near_to)
    t_f1 = copy_to(tb.at[0, NEAR, h1], tf.at[0, h1], pair)
    i_o0 = copy_to(ib.at[LEFT, h0], ib.at[OPP, h0], right)
    i_o1 = copy_to(ib.at[RIGHT, h1], ib.at[OPP, h1], left)
    s_p0 = copy_to(tb.at[0, PAIR, h0], tb.at[1, PAIR, h0], sibling)
    s_n1 = copy_to(tb.at[0, NEAR, h1], tb.at[1, NEAR, h1], sibling)
    s_p1 = copy_to(tb.at[0, PAIR, h1], tb.at[1, PAIR, h1], sibling)
    s_n0 = copy_to(tb.at[0, NEAR, h0], tb.at[1, NEAR, h0], sibling)
    s_f0 = copy_to(tf.at[0, h0], tf.at[1, h0], sibling)
    s_f1 = copy_to(tf.at[0, h1], tf.at[1, h1], sibling)

    load_s.wait()
    load_b.wait()
    temper = jnp.exp(jnp.full((1, 1), ls_ref[0], F32))
    offset = bi_ref[0]
    loss[...] = jnp.zeros_like(loss)

    def score(name, chunk, weights, lo, hi, pairs=False):
        with jax.named_scope("score_" + name):
            n, m = chunk.shape[0], (hi - lo) * rows
            dots = lax.dot_general(chunk, ib[lo:hi].reshape(m, width),
                                   (((1,), (1,)), ((), ())), preferred_element_type=F32)
            logit = temper * dots + offset
            e = jnp.exp(-jnp.abs(logit))
            weight = jnp.where(logit >= 0, 1.0, e) * pl.reciprocal(1.0 + e, approx=True)
            signed = logit
            if pairs:
                r = lax.broadcasted_iota(jnp.int32, logit.shape, 0)
                paired = (r == lax.broadcasted_iota(jnp.int32, logit.shape, 1)) & (r < rows)
                weight = weight - paired.astype(F32)
                signed = jnp.where(paired, -logit, logit)
            weights[:, pl.ds(lo * rows, m)] = (temper * weight).astype(BF)
            e = e.reshape(n // (8 * GROUP), GROUP, 8, m)
            p = e[:, 0]
            for g in range(1, GROUP):
                p = p + e[:, g] * (1.0 + p)
            log1p = jnp.where(p < 1e-3, p * (1.0 - 0.5 * p), jnp.log(1.0 + p))
            lost = (jnp.sum(jnp.maximum(signed, 0.0).reshape(n // 8, 8, m), axis=0)
                    + jnp.sum(log1p, axis=0))
            for slot in range(lo, hi):
                loss[slot] += lost[:, (slot - lo) * rows:(slot - lo + 1) * rows]

    def score_main(kk, lo, hi):
        score(f"main_{kk}_{lo}_{hi}", tb[kk].reshape(3 * rows, width),
              coef.at[pl.ds(kk * 3 * rows, 3 * rows)], lo, hi, pairs=kk == 0 and lo == 0)

    def score_far(kk):
        score(f"far_{kk}", tf[kk], coef_f.at[pl.ds(kk * rows, rows)], 0, OPP + 1)

    def image_partial(lo, hi):
        turned = (((0,), (0,)), ((), ()))
        cols = pl.ds(lo * rows, (hi - lo) * rows)
        return (lax.dot_general(coef[:, cols], tb[...].reshape(6 * rows, width), turned,
                                preferred_element_type=F32)
                + lax.dot_general(coef_f[:, cols], tf[...].reshape(2 * rows, width), turned,
                                  preferred_element_type=F32))

    arrived("first_p", t_p0)
    t_f0.start()
    s_p0.start()
    arrived("first_i", i_r0, i_l1)
    i_o0.start()
    i_o1.start()
    arrived("first_n", t_n1)
    t_f1.start()
    s_n1.start()
    arrived("second_p", t_p1)
    s_p1.start()
    arrived("second_n", t_n0)
    s_n0.start()
    arrived("second_i", i_r1, i_l0)
    score_main(0, 0, OPP)
    arrived("main_sibling", s_own, s_p0, s_n1, s_p1, s_n0)
    score_main(1, 0, OPP)
    arrived("opp_i", i_o0, i_o1)
    score_main(0, OPP, OPP + 1)
    score_main(1, OPP, OPP + 1)
    arrived("far_t0", t_f0)
    s_f0.start()
    arrived("far_t1", t_f1)
    s_f1.start()
    score_far(0)
    arrived("far_sibling", s_f0, s_f1)
    score_far(1)

    back = [copy_to(sib_out.at[s], sib_in.at[s], sibling) for s in range(4)]
    f_p0 = copy_to(t_out.at[FAR - 1, h0], t_mid.at[0], pair)
    f_n1 = copy_to(t_out.at[FAR - 1, h1], t_mid.at[1], near_of)
    b_p0 = copy_to(t_out.at[PAIR - 1, h0], t_in.at[0, h0], pair)
    b_p1 = copy_to(t_out.at[PAIR - 1, h1], t_in.at[0, h1], pair)
    b_n1 = copy_to(t_out.at[NEAR - 1, h1], t_in.at[1, h1], near_of)
    b_n0 = copy_to(t_out.at[NEAR - 1, h0], t_in.at[1, h0], near_of)
    f_r0 = copy_to(i_out.at[OPP - 1, h0], i_mid.at[0], right)
    f_l1 = copy_to(i_out.at[OPP - 1, h1], i_mid.at[1], left)
    b_r1 = copy_to(i_out.at[RIGHT - 1, h1], i_in.at[0, h1], right)
    b_r0 = copy_to(i_out.at[RIGHT - 1, h0], i_in.at[0, h0], right)
    b_l0 = copy_to(i_out.at[LEFT - 1, h0], i_in.at[1, h0], left)
    b_l1 = copy_to(i_out.at[LEFT - 1, h1], i_in.at[1, h1], left)
    l_o = copy_to(loss.at[OPP], l_mid, right)
    l_r = copy_to(loss.at[RIGHT], l_in.at[0], right)
    l_l = copy_to(loss.at[LEFT], l_in.at[1], left)

    all_images = ib[...].reshape(4 * rows, width)

    def text_partial(weights):
        return jnp.dot(weights, all_images, preferred_element_type=F32)

    def add_sibling(s, part):
        arrived(f"text_sibling_{s}", back[s])
        return part + sib_in[s].astype(F32)

    l_o.start()
    with jax.named_scope("image_opp"):
        i_out[OPP - 1] = image_partial(OPP, OPP + 1).astype(BF)
        f_r0.start()
        f_l1.start()
    with jax.named_scope("text_far_1"):
        sib_out[FAR] = text_partial(coef_f[rows:]).astype(BF)
        back[FAR].start()
    l_l.start()
    with jax.named_scope("text_far_0"):
        far = text_partial(coef_f[:rows])
    t_out[FAR - 1] = add_sibling(FAR, far).astype(BF)
    f_p0.start()
    f_n1.start()
    with jax.named_scope("text_main_1"):
        sib_out[OWN:FAR] = text_partial(coef[3 * rows:]).astype(BF).reshape(3, rows, width)
        for s in (PAIR, NEAR, OWN):
            back[s].start()
    with jax.named_scope("image_next"):
        i_out[RIGHT - 1:LEFT] = image_partial(RIGHT, LEFT + 1).astype(BF).reshape(2, rows, width)
        b_r1.start()
        b_l0.start()
    with jax.named_scope("text_main_0"):
        main = text_partial(coef[:3 * rows])
        gt[...] = main[:rows]
    t_out[PAIR - 1] = add_sibling(PAIR, main[rows:2 * rows]).astype(BF)
    b_p0.start()
    t_out[NEAR - 1] = add_sibling(NEAR, main[2 * rows:]).astype(BF)
    b_n1.start()
    with jax.named_scope("image_own"):
        gi[...] = image_partial(0, 1)

    def pass_on(name, got, src, slot, part, middle):
        arrived(name, got)
        src[slot, part] = (src[slot, part].astype(F32) + middle[...].astype(F32)).astype(BF)

    arrived("mid_loss", l_o)
    loss[RIGHT] += l_mid[...]
    l_r.start()
    pass_on("mid_r", f_r0, i_out, RIGHT - 1, h0, i_mid.at[0])
    b_r0.start()
    pass_on("mid_l", f_l1, i_out, LEFT - 1, h1, i_mid.at[1])
    b_l1.start()
    pass_on("mid_n", f_p0, t_out, NEAR - 1, h0, t_mid.at[0])
    b_n0.start()
    pass_on("mid_p", f_n1, t_out, PAIR - 1, h1, t_mid.at[1])
    b_p1.start()
    gt[...] = add_sibling(OWN, gt[...])

    def backnorm(values, inverse, grad):
        unit = values * inverse
        return inverse * (grad - unit * jnp.sum(unit * grad, axis=1, keepdims=True))

    arrived("loss", l_r, l_l)
    total = loss[0] + l_in[0] + l_in[1]
    row[...] = jnp.sum(total, axis=0, keepdims=True) / mean
    puts = [pltpu.make_async_copy(held, out, lsem.at[i])
            for i, (held, out) in enumerate(((row, loss_hbm), (gi, gi_hbm), (gt, gt_hbm)))]
    puts[0].start()
    arrived("image_back", b_r1, b_l0, b_r0, b_l1)
    with jax.named_scope("image_norm"):
        grad = gi[...] + i_in[0].astype(F32) + i_in[1].astype(F32)
        gi[...] = backnorm(img[...], inv_i, grad)
        puts[1].start()
    arrived("text_back", b_p0, b_n1, b_n0, b_p1)
    with jax.named_scope("text_norm"):
        grad = gt[...] + t_in[0].astype(F32) + t_in[1].astype(F32)
        gt[...] = backnorm(txt[...], inv_t, grad)
        puts[2].start()
    with jax.named_scope("sends_end"):
        for c in sent:
            c.wait_send()
    with jax.named_scope("put"):
        for c in puts:
            c.wait()


def hand_on(row, gi, gt, row_out, gi_out, gt_out, row_held, gi_held, gt_held, in_sem, out_sem):
    parts = [(row, row_held, row_out)]
    size = gi.shape[0] // PARTS
    for at in range(0, gi.shape[0], size):
        for src, held, out in ((gi, gi_held, gi_out), (gt, gt_held, gt_out)):
            parts.append(tuple(ref.at[pl.ds(at, size)] for ref in (src, held, out)))
    reads = [pltpu.make_async_copy(src, held, in_sem.at[i]) for i, (src, held, _) in enumerate(parts)]
    writes = [pltpu.make_async_copy(held, out, out_sem.at[i]) for i, (_, held, out) in enumerate(parts)]
    for c in reads:
        c.start()
    for r, w in zip(reads, writes):
        r.wait()
        w.start()
    for c in writes:
        c.wait()


def body(images, texts, log_scale, bias):
    rows, width = images.shape
    n_blk = lax.axis_size("blk")
    mean = STEPS * rows * lax.axis_size("grp")
    low = functools.partial(pltpu.VMEM, dtype=BF)
    full = functools.partial(pltpu.VMEM, dtype=F32)
    anywhere = pl.BlockSpec(memory_space=pl.ANY)
    results = (
        jax.ShapeDtypeStruct((1, rows), F32),
        jax.ShapeDtypeStruct((rows, width), F32),
        jax.ShapeDtypeStruct((rows, width), F32),
    )
    held = pl.pallas_call(
        functools.partial(kernel, n_blk, mean),
        out_shape=results,
        in_specs=[anywhere] * 4,
        out_specs=(anywhere,) * 3,
        scratch_shapes=[
            pltpu.SMEM((1,), F32), pltpu.SMEM((1,), F32),
            full((rows, width)), full((rows, width)),
            full((rows, width)), full((rows, width)), full((1, rows)),
            low((4, rows, width)),
            low((2, 3, rows, width)), low((2, rows, width)),
            low((6 * rows, 4 * rows)), low((2 * rows, 4 * rows)),
            full((4, 8, rows)),
            low((4, rows, width)), low((4, rows, width)),
            low((3, rows, width)), low((2, rows // 2, width)), low((2, rows, width)),
            low((3, rows, width)), low((2, rows // 2, width)), low((2, rows, width)),
            full((8, rows)), full((2, 8, rows)),
            pltpu.SemaphoreType.DMA((4,)),
            pltpu.SemaphoreType.DMA((N_SEMS,)),
            pltpu.SemaphoreType.DMA((N_SEMS,)),
        ],
        compiler_params=pltpu.CompilerParams(
            collective_id=0, has_side_effects=True, vmem_limit_bytes=(64 << 20) - (1 << 19)),
        name="pair_loss",
    )(log_scale, bias, images, texts)
    row_loss, image_grad, text_grad = pl.pallas_call(
        hand_on,
        out_shape=results,
        in_specs=[anywhere] * 3,
        out_specs=(anywhere,) * 3,
        scratch_shapes=[
            full((1, rows)), full((rows, width)), full((rows, width)),
            pltpu.SemaphoreType.DMA((2 * PARTS + 1,)), pltpu.SemaphoreType.DMA((2 * PARTS + 1,)),
        ],
        name="hand_on",
    )(*held)
    return row_loss.reshape(rows), image_grad, text_grad


def solution(mesh):
    in_specs = (P(("blk", "grp"), None), P(("blk", "grp"), None), P(), P())
    out_specs = (P(("blk", "grp")), P(("blk", "grp"), None), P(("blk", "grp"), None))
    return jax.shard_map(body, mesh=mesh, in_specs=in_specs, out_specs=out_specs, check_vma=False)
```

time: 50.9 us -> 48.4 us (0.951)
  local copies, waits for them, and re-layouts: 3.92 us -> 0 us
  Pallas kernels: 44.9 us -> 46.3 us
    unnamed x7 -> x0, local copies, waits for them, and re-layouts: 3.92 us -> none
    pallas_call x1 -> x2, Pallas kernels: 44.9 us -> 46.3 us  [the longest x1 44.1 us: body(): pl.pallas_call(functools.partial(kernel, n_blk, mean), out_shape=results,...]
where the time goes in v3:
time: 48.4 us; the launch traced here: 48.2 us
  Pallas kernels  46.3 us (96%)
  between operations  1.93 us (4%)
    pallas_call x1, Pallas kernels, body(): pl.pallas_call(functools.partial(kernel, n_blk, mean), out_shape=results,...  44.1 us
    pallas_call x1, Pallas kernels, body(): pl.pallas_call(hand_on, out_shape=results, in_specs=[anywhere] * 3, out_s...  2.17 us

profile of v3, /device:TPU:1, one launch (start us, length us, event | category | flops | bytes accessed | tf_op | source)
XLA Modules:
  0.0 48.2 jit_solution(10119152184516937986)
XLA Ops:
  1.9 44.1 %pair_loss.1 = (f32[1,128]{1,0:T(1,128)}, f32[128,1152]{1,0:T(8,128)}, f32[128,1152]{1,0:T(8,128)}) custom-call(f32[1]{0:T(128)S(6)} %copy.7.ls_hbm, f32[1]{0:T(128)S(6)} %copy.8.bi_hbm, f32[128,1152]{1,0:T(8,128)} %img_hbm.1, f32[128,1152]{1,0:T(8,128)} %txt_hbm.1), custom_call_target="tpu_custom_call" | custom-call | tf_op jit(solution)/shard_map/pair_loss/pallas_call | solution.py:321
  46.1 2.2 %hand_on.1 = (f32[1,128]{1,0:T(1,128)}, f32[128,1152]{1,0:T(8,128)}, f32[128,1152]{1,0:T(8,128)}) custom-call(f32[1,128]{1,0:T(1,128)} %get-tuple-element.9.row, f32[128,1152]{1,0:T(8,128)} %get-tuple-element.10.gi, f32[128,1152]{1,0:T(8,128)} %get-tuple-element.11.gt), custom_call_target="tpu_custom_call" | custom-call | tf_op jit(solution)/shard_map/hand_on/pallas_call | solution.py:346

commit v4 on v3

v4 whole, which is shorter than its diff:
```python
import functools

import jax
import jax.numpy as jnp
from jax import lax
from jax.experimental import pallas as pl
from jax.experimental.pallas import tpu as pltpu
from jax.sharding import PartitionSpec as P

STEPS = 2
MESH = pl.DeviceIdType.MESH
BF = jnp.bfloat16
F32 = jnp.float32
N_SEMS = 44
GROUP = 16
PARTS = 4

OWN0, PAIR0, OWN1, PAIR1, NEAR0, NEAR1, FAR0, FAR1 = range(8)
OWN, PAIR, NEAR, FAR = range(4)
RIGHT, LEFT, OPP = 1, 2, 3


def places(n_blk):
    b = lax.axis_index("blk")
    g = lax.axis_index("grp")
    core = lax.rem(g, 2)
    x_lo = lax.rem(g // 2, 2)
    y = g // 4
    nxt = lax.rem(b + 1, n_blk)
    prv = lax.rem(b + n_blk - 1, n_blk)

    def member(yy, xx, kk):
        return (yy * 2 + xx) * 2 + kk

    sibling = (b, member(y, x_lo, 1 - core))
    pair = (b, member(y, 1 - x_lo, core))
    near_to = (nxt, member(y, 1 - x_lo, core))
    near_of = (prv, member(y, 1 - x_lo, core))
    right = (b, member(lax.rem(y + 1, 4), x_lo, core))
    left = (b, member(lax.rem(y + 3, 4), x_lo, core))
    return sibling, pair, near_to, near_of, right, left


def inverse_norm(values):
    return lax.rsqrt(jnp.sum(values * values, axis=1, keepdims=True) + 1e-06)


def kernel(n_blk, mean, ls_hbm, bi_hbm, img_hbm, txt_hbm, loss_hbm, gi_hbm, gt_hbm,
           ls_ref, bi_ref, img, txt, gi, gt, row, kept, ib, tb, coef, loss, sib_out, sib_in,
           t_out, t_mid, t_in, i_out, i_mid, i_in, l_mid, l_in, lsem, ssem, rsem):
    rows, width = img.shape
    half = rows // 2
    h0, h1 = pl.ds(0, half), pl.ds(half, half)
    quarters = [pl.ds(at, half // 2) for at in range(0, rows, half // 2)]
    blk = lax.axis_index("blk")
    sibling, pair, near_to, near_of, right, left = places(n_blk)
    barrier = pltpu.get_barrier_semaphore()
    others = [sibling, pair, near_of, right, left]
    for other in others:
        pl.semaphore_signal(barrier, inc=1, device_id=other, device_id_type=MESH)

    load_t = pltpu.make_async_copy(txt_hbm, txt, lsem.at[0])
    load_i = pltpu.make_async_copy(img_hbm, img, lsem.at[1])
    load_t.start()
    load_i.start()
    load_s = pltpu.make_async_copy(ls_hbm, ls_ref, lsem.at[2])
    load_b = pltpu.make_async_copy(bi_hbm, bi_ref, lsem.at[3])
    load_s.start()
    load_b.start()

    sent = []

    def copy_to(src, dst, to):
        s = len(sent)
        copy = pltpu.make_async_remote_copy(
            src_ref=src, dst_ref=dst, send_sem=ssem.at[s], recv_sem=rsem.at[s],
            device_id=to, device_id_type=MESH)
        sent.append(copy)
        return copy

    def arrived(name, *copies):
        with jax.named_scope("wait_" + name):
            for c in copies:
                c.wait_recv()

    with jax.named_scope("normalize_text"):
        load_t.wait()
        inv_t = inverse_norm(txt[...])
        tb[OWN0] = (txt[...] * inv_t).astype(BF)
    with jax.named_scope("barrier"):
        pl.semaphore_wait(barrier, len(others))

    t_p0 = copy_to(tb.at[OWN0, h0], tb.at[PAIR0, h0], pair)
    t_n = [copy_to(tb.at[OWN0, q], tb.at[NEAR0, q], near_to) for q in quarters]
    t_p1 = copy_to(tb.at[OWN0, h1], tb.at[PAIR0, h1], pair)
    s_own = copy_to(tb.at[OWN0], tb.at[OWN1], sibling)
    for c in (t_n[3], t_p0, t_n[2], t_p1, t_n[1], t_n[0], s_own):
        c.start()
    with jax.named_scope("normalize_image"):
        load_i.wait()
        inv_i = inverse_norm(img[...])
        ib[0] = (img[...] * inv_i).astype(BF)
    i_r0 = copy_to(ib.at[0, h0], ib.at[LEFT, h0], right)
    i_l1 = copy_to(ib.at[0, h1], ib.at[RIGHT, h1], left)
    i_r1 = copy_to(ib.at[0, h1], ib.at[LEFT, h1], right)
    i_l0 = copy_to(ib.at[0, h0], ib.at[RIGHT, h0], left)
    for c in (i_r0, i_l1, i_r1, i_l0):
        c.start()
    i_o0 = copy_to(ib.at[LEFT, h0], ib.at[OPP, h0], right)
    i_o1 = copy_to(ib.at[RIGHT, h1], ib.at[OPP, h1], left)
    s_p0 = copy_to(tb.at[PAIR0, h0], tb.at[PAIR1, h0], sibling)
    s_n1 = copy_to(tb.at[NEAR0, h1], tb.at[NEAR1, h1], sibling)
    s_p1 = copy_to(tb.at[PAIR0, h1], tb.at[PAIR1, h1], sibling)
    s_n0 = copy_to(tb.at[NEAR0, h0], tb.at[NEAR1, h0], sibling)
    s_f0 = copy_to(tb.at[FAR0, h0], tb.at[FAR1, h0], sibling)
    s_f1 = copy_to(tb.at[FAR0, h1], tb.at[FAR1, h1], sibling)
    t_f0 = copy_to(tb.at[PAIR0, h0], tb.at[FAR0, h0], near_to)
    t_f1 = copy_to(tb.at[NEAR0, h1], tb.at[FAR0, h1], pair)
    t_q = ([copy_to(tb.at[PAIR0, quarters[0]], tb.at[FAR0, quarters[0]], near_to)]
           + [copy_to(tb.at[NEAR0, q], tb.at[FAR0, q], pair) for q in quarters[1:]])
    into_first = blk == n_blk - 1
    first = blk == 0

    load_s.wait()
    load_b.wait()
    temper = jnp.exp(jnp.full((1, 1), ls_ref[0], F32))
    offset = bi_ref[0]
    loss[...] = jnp.zeros_like(loss)

    def score(first, last, lo, hi):
        with jax.named_scope(f"score_{first}_{last}_{lo}_{hi}"):
            n, m = (last - first) * rows, (hi - lo) * rows
            dots = lax.dot_general(tb[first:last].reshape(n, width), ib[lo:hi].reshape(m, width),
                                   (((1,), (1,)), ((), ())), preferred_element_type=F32)
            logit = temper * dots + offset
            e = jnp.exp(-jnp.abs(logit))
            weight = jnp.where(logit >= 0, 1.0, e) * pl.reciprocal(1.0 + e, approx=True)
            signed = logit
            if first == OWN0 and lo == 0:
                r = lax.broadcasted_iota(jnp.int32, logit.shape, 0)
                paired = (r == lax.broadcasted_iota(jnp.int32, logit.shape, 1)) & (r < rows)
                weight = weight - paired.astype(F32)
                signed = jnp.where(paired, -logit, logit)
            coef[pl.ds(first * rows, n), pl.ds(lo * rows, m)] = (temper * weight).astype(BF)
            e = e.reshape(n // (8 * GROUP), GROUP, 8, m)
            p = e[:, 0]
            for g in range(1, GROUP):
                p = p + e[:, g] * (1.0 + p)
            log1p = jnp.where(p < 1e-3, p * (1.0 - 0.5 * p), jnp.log(1.0 + p))
            lost = (jnp.sum(jnp.maximum(signed, 0.0).reshape(n // 8, 8, m), axis=0)
                    + jnp.sum(log1p, axis=0))
            for slot in range(lo, hi):
                loss[slot] += lost[:, (slot - lo) * rows:(slot - lo + 1) * rows]

    def image_partial(lo, hi, first, last):
        return lax.dot_general(coef[first * rows:last * rows, lo * rows:hi * rows],
                               tb[first:last].reshape((last - first) * rows, width),
                               (((0,), (0,)), ((), ())), preferred_element_type=F32)

    back = [copy_to(sib_out.at[s], sib_in.at[s], sibling) for s in range(4)]
    f_p0 = copy_to(t_out.at[FAR - 1, h0], t_mid.at[0], pair)
    f_n1 = copy_to(t_out.at[FAR - 1, h1], t_mid.at[1], near_of)
    b_p0 = copy_to(t_out.at[PAIR - 1, h0], t_in.at[0, h0], pair)
    b_p1 = copy_to(t_out.at[PAIR - 1, h1], t_in.at[0, h1], pair)
    b_n1 = copy_to(t_out.at[NEAR - 1, h1], t_in.at[1, h1], near_of)
    b_n0 = copy_to(t_out.at[NEAR - 1, h0], t_in.at[1, h0], near_of)
    f_r0 = copy_to(i_out.at[OPP - 1, h0], i_mid.at[0], right)
    f_l1 = copy_to(i_out.at[OPP - 1, h1], i_mid.at[1], left)
    b_r1 = copy_to(i_out.at[RIGHT - 1, h1], i_in.at[0, h1], right)
    b_r0 = copy_to(i_out.at[RIGHT - 1, h0], i_in.at[0, h0], right)
    b_l0 = copy_to(i_out.at[LEFT - 1, h0], i_in.at[1, h0], left)
    b_l1 = copy_to(i_out.at[LEFT - 1, h1], i_in.at[1, h1], left)
    l_o = copy_to(loss.at[OPP], l_mid, right)
    l_r = copy_to(loss.at[RIGHT], l_in.at[0], right)
    l_l = copy_to(loss.at[LEFT], l_in.at[1], left)

    def text_partial(first, last):
        return jnp.dot(coef[first * rows:last * rows], ib[...].reshape(4 * rows, width),
                       preferred_element_type=F32)

    def to_sibling(s, part):
        sib_out[s] = part.astype(BF)
        back[s].start()

    def add_sibling(s, part):
        arrived(f"text_sibling_{s}", back[s])
        return part + sib_in[s].astype(F32)

    def pass_on(name, got, src, slot, part, middle, out):
        arrived(name, got)
        src[slot, part] = (src[slot, part].astype(F32) + middle[...].astype(F32)).astype(BF)
        out.start()

    def pass_loss():
        arrived("mid_loss", l_o)
        loss[RIGHT] += l_mid[...]
        l_r.start()

    def pass_right():
        pass_on("mid_r", f_r0, i_out, RIGHT - 1, h0, i_mid.at[0], b_r0)

    def pass_left():
        pass_on("mid_l", f_l1, i_out, LEFT - 1, h1, i_mid.at[1], b_l1)

    def pass_near():
        pass_on("mid_n", f_p0, t_out, NEAR - 1, h0, t_mid.at[0], b_n0)

    def pass_pair():
        pass_on("mid_p", f_n1, t_out, PAIR - 1, h1, t_mid.at[1], b_p1)

    puts = [pltpu.make_async_copy(held, out, lsem.at[i])
            for i, (held, out) in enumerate(((row, loss_hbm), (gi, gi_hbm), (gt, gt_hbm)))]

    def backnorm(values, inverse, grad):
        unit = values * inverse
        return inverse * (grad - unit * jnp.sum(unit * grad, axis=1, keepdims=True))

    def finish_loss():
        arrived("loss", l_r, l_l)
        total = loss[0] + l_in[0] + l_in[1]
        row[...] = jnp.sum(total, axis=0, keepdims=True) / mean
        puts[0].start()

    def finish_image():
        arrived("image_back", b_r1, b_l0, b_r0, b_l1)
        with jax.named_scope("image_norm"):
            grad = gi[...] + i_in[0].astype(F32) + i_in[1].astype(F32)
            gi[...] = backnorm(img[...], inv_i, grad)
            puts[1].start()

    def finish_text():
        arrived("text_back", b_p0, b_n1, b_n0, b_p1)
        with jax.named_scope("text_norm"):
            grad = gt[...] + t_in[0].astype(F32) + t_in[1].astype(F32)
            gt[...] = backnorm(txt[...], inv_t, grad)
            puts[2].start()

    def start_own_plane():
        arrived("first_p", t_p0)
        pl.when(into_first)(t_q[0].start)
        pl.when(jnp.logical_not(into_first))(t_f0.start)
        s_p0.start()
        arrived("first_i", i_r0, i_l1)
        i_o0.start()
        i_o1.start()

    @pl.when(jnp.logical_not(first))
    def _():
        start_own_plane()
        arrived("first_n", t_n[3], t_n[2])
        t_f1.start()
        s_n1.start()
        arrived("second_p", t_p1)
        s_p1.start()
        arrived("second_n", t_n[1], t_n[0])
        s_n0.start()
        arrived("second_i", i_r1, i_l0)
        score(OWN0, OWN1, 0, OPP)
        arrived("pair_sibling", s_own, s_p0, s_p1)
        score(OWN1, NEAR0, 0, OPP)
        arrived("near_sibling", s_n1, s_n0)
        score(NEAR0, FAR0, 0, OPP)
        arrived("far_t0", t_f0)
        s_f0.start()
        arrived("far_t1", t_f1)
        s_f1.start()
        arrived("opp_i", i_o0, i_o1)
        score(OWN0, FAR0, OPP, OPP + 1)
        score(FAR0, FAR1, 0, OPP + 1)
        arrived("far_sibling", s_f0, s_f1)
        score(FAR1, FAR1 + 1, 0, OPP + 1)
        l_o.start()
        l_l.start()
        with jax.named_scope("text_far_1"):
            to_sibling(FAR, text_partial(FAR1, FAR1 + 1))
        with jax.named_scope("image_opp"):
            i_out[OPP - 1] = image_partial(OPP, OPP + 1, OWN0, FAR1 + 1).astype(BF)
            f_r0.start()
            f_l1.start()
        with jax.named_scope("text_far_0"):
            t_out[FAR - 1] = add_sibling(FAR, text_partial(FAR0, FAR1)).astype(BF)
            f_p0.start()
            f_n1.start()
        with jax.named_scope("text_mid"):
            mid = text_partial(OWN1, FAR0)
            to_sibling(PAIR, mid[rows:2 * rows])
            to_sibling(NEAR, mid[3 * rows:])
            to_sibling(OWN, mid[:rows])
            near = mid[2 * rows:3 * rows]
        with jax.named_scope("image_next"):
            part = image_partial(RIGHT, LEFT + 1, OWN0, FAR1 + 1)
            i_out[RIGHT - 1:LEFT] = part.astype(BF).reshape(2, rows, width)
            b_r1.start()
            b_l0.start()
        with jax.named_scope("text_near"):
            t_out[NEAR - 1] = add_sibling(NEAR, near).astype(BF)
            b_n1.start()
        with jax.named_scope("text_own"):
            own = text_partial(OWN0, OWN1)
            t_out[PAIR - 1] = add_sibling(PAIR, own[rows:]).astype(BF)
            b_p0.start()
            gt[...] = own[:rows]
        with jax.named_scope("image_own"):
            gi[...] = image_partial(0, 1, OWN0, FAR1 + 1)
        pass_loss()
        pass_right()
        pass_left()
        pass_near()
        pass_pair()
        gt[...] = add_sibling(OWN, gt[...])
        finish_loss()
        finish_image()
        finish_text()

    @pl.when(first)
    def _():
        start_own_plane()
        arrived("second_p", t_p1)
        s_p1.start()
        arrived("second_i", i_r1, i_l0)
        score(OWN0, OWN1, 0, OPP)
        arrived("pair_sibling", s_own, s_p0, s_p1)
        score(OWN1, NEAR0, 0, OPP)
        arrived("opp_i", i_o0, i_o1)
        score(OWN0, NEAR0, OPP, OPP + 1)
        arrived("first_n", t_n[3])
        t_q[3].start()
        arrived("second_n", t_n[2])
        t_q[2].start()
        s_n1.start()
        arrived("third_n", t_n[1])
        t_q[1].start()
        with jax.named_scope("text_block"):
            part = text_partial(OWN0, NEAR0)
            to_sibling(PAIR, part[3 * rows:])
            to_sibling(OWN, part[2 * rows:3 * rows])
            gt[...] = part[:rows]
            kept[...] = part[rows:2 * rows]
        arrived("last_n", t_n[0])
        s_n0.start()
        score(NEAR0, NEAR1, 0, OPP + 1)
        arrived("near_sibling", s_n1, s_n0)
        score(NEAR1, FAR0, 0, OPP + 1)
        arrived("far_t1", t_q[3], t_q[2])
        s_f1.start()
        arrived("far_t0", t_q[0], t_q[1])
        s_f0.start()
        score(FAR0, FAR1, 0, OPP + 1)
        with jax.named_scope("image_ahead"):
            gi[...] = image_partial(OPP, OPP + 1, OWN0, FAR0)
        t_out[PAIR - 1] = add_sibling(PAIR, kept[...]).astype(BF)
        b_p0.start()
        arrived("far_sibling", s_f0, s_f1)
        score(FAR1, FAR1 + 1, 0, OPP + 1)
        l_o.start()
        l_l.start()
        with jax.named_scope("image_opp"):
            i_out[OPP - 1] = (gi[...] + image_partial(OPP, OPP + 1, FAR0, FAR1 + 1)).astype(BF)
            f_r0.start()
            f_l1.start()
        with jax.named_scope("text_far"):
            part = text_partial(NEAR0, FAR1 + 1)
            to_sibling(FAR, part[3 * rows:])
            to_sibling(NEAR, part[rows:2 * rows])
            kept[...] = part[2 * rows:3 * rows]
            near = part[:rows]
        with jax.named_scope("image_next"):
            part = image_partial(RIGHT, OPP, OWN0, FAR1 + 1)
            i_out[RIGHT - 1:LEFT] = part.astype(BF).reshape(2, rows, width)
            b_r1.start()
            b_l0.start()
        t_out[FAR - 1] = add_sibling(FAR, kept[...]).astype(BF)
        f_p0.start()
        f_n1.start()
        t_out[NEAR - 1] = add_sibling(NEAR, near).astype(BF)
        b_n1.start()
        pass_pair()
        gt[...] = add_sibling(OWN, gt[...])
        with jax.named_scope("image_own"):
            gi[...] = image_partial(0, 1, OWN0, FAR1 + 1)
        pass_loss()
        pass_right()
        pass_left()
        pass_near()
        finish_loss()
        finish_text()
        finish_image()

    with jax.named_scope("sends_end"):
        for c in sent:
            if not any(c is o for o in (t_f0, t_f1, *t_q)):
                c.wait_send()
        pl.when(into_first)(t_q[0].wait_send)
        pl.when(jnp.logical_not(into_first))(t_f0.wait_send)
        pl.when(jnp.logical_not(first))(t_f1.wait_send)
        for c in t_q[1:]:
            pl.when(first)(c.wait_send)
    with jax.named_scope("put"):
        for c in puts:
            c.wait()


def hand_on(row, gi, gt, row_out, gi_out, gt_out, row_held, gi_held, gt_held, in_sem, out_sem):
    parts = [(row, row_held, row_out)]
    size = gi.shape[0] // PARTS
    for at in range(0, gi.shape[0], size):
        for src, held, out in ((gi, gi_held, gi_out), (gt, gt_held, gt_out)):
            parts.append(tuple(ref.at[pl.ds(at, size)] for ref in (src, held, out)))
    reads = [pltpu.make_async_copy(src, held, in_sem.at[i]) for i, (src, held, _) in enumerate(parts)]
    writes = [pltpu.make_async_copy(held, out, out_sem.at[i]) for i, (_, held, out) in enumerate(parts)]
    for c in reads:
        c.start()
    for r, w in zip(reads, writes):
        r.wait()
        w.start()
    for c in writes:
        c.wait()


def body(images, texts, log_scale, bias):
    rows, width = images.shape
    n_blk = lax.axis_size("blk")
    mean = STEPS * rows * lax.axis_size("grp")
    low = functools.partial(pltpu.VMEM, dtype=BF)
    full = functools.partial(pltpu.VMEM, dtype=F32)
    anywhere = pl.BlockSpec(memory_space=pl.ANY)
    results = (
        jax.ShapeDtypeStruct((1, rows), F32),
        jax.ShapeDtypeStruct((rows, width), F32),
        jax.ShapeDtypeStruct((rows, width), F32),
    )
    held = pl.pallas_call(
        functools.partial(kernel, n_blk, mean),
        out_shape=results,
        in_specs=[anywhere] * 4,
        out_specs=(anywhere,) * 3,
        scratch_shapes=[
            pltpu.SMEM((1,), F32), pltpu.SMEM((1,), F32),
            full((rows, width)), full((rows, width)),
            full((rows, width)), full((rows, width)), full((1, rows)),
            full((rows, width)),
            low((4, rows, width)),
            low((8, rows, width)),
            low((8 * rows, 4 * rows)),
            full((4, 8, rows)),
            low((4, rows, width)), low((4, rows, width)),
            low((3, rows, width)), low((2, rows // 2, width)), low((2, rows, width)),
            low((3, rows, width)), low((2, rows // 2, width)), low((2, rows, width)),
            full((8, rows)), full((2, 8, rows)),
            pltpu.SemaphoreType.DMA((4,)),
            pltpu.SemaphoreType.DMA((N_SEMS,)),
            pltpu.SemaphoreType.DMA((N_SEMS,)),
        ],
        compiler_params=pltpu.CompilerParams(
            collective_id=0, has_side_effects=True, vmem_limit_bytes=(64 << 20) - (1 << 19)),
        name="pair_loss",
    )(log_scale, bias, images, texts)
    row_loss, image_grad, text_grad = pl.pallas_call(
        hand_on,
        out_shape=results,
        in_specs=[anywhere] * 3,
        out_specs=(anywhere,) * 3,
        scratch_shapes=[
            full((1, rows)), full((rows, width)), full((rows, width)),
            pltpu.SemaphoreType.DMA((2 * PARTS + 1,)), pltpu.SemaphoreType.DMA((2 * PARTS + 1,)),
        ],
        name="hand_on",
    )(*held)
    return row_loss.reshape(rows), image_grad, text_grad


def solution(mesh):
    in_specs = (P(("blk", "grp"), None), P(("blk", "grp"), None), P(), P())
    out_specs = (P(("blk", "grp")), P(("blk", "grp"), None), P(("blk", "grp"), None))
    return jax.shard_map(body, mesh=mesh, in_specs=in_specs, out_specs=out_specs, check_vma=False)
```

time: 48.4 us -> 46.3 us (0.957)
  Pallas kernels: 46.3 us -> 44.1 us
    pallas_call x1, Pallas kernels: 44.1 us -> 41.9 us  [body(): pl.pallas_call(functools.partial(kernel, n_blk, mean), out_shape=results,...]
where the time goes in v4:
time: 46.3 us; the launch traced here: 46.1 us
  Pallas kernels  44.1 us (95%)
  between operations  2.09 us (5%)
    pallas_call x1, Pallas kernels, body(): pl.pallas_call(functools.partial(kernel, n_blk, mean), out_shape=results,...  41.9 us
    pallas_call x1, Pallas kernels, body(): pl.pallas_call(hand_on, out_shape=results, in_specs=[anywhere] * 3, out_s...  2.17 us

profile of v4, /device:TPU:1, one launch (start us, length us, event | category | flops | bytes accessed | tf_op | source)
XLA Modules:
  0.0 46.1 jit_solution(3763707618559367553)
XLA Ops:
  1.9 41.9 %pair_loss.1 = (f32[1,128]{1,0:T(1,128)}, f32[128,1152]{1,0:T(8,128)}, f32[128,1152]{1,0:T(8,128)}) custom-call(f32[1]{0:T(128)S(6)} %copy.7.ls_hbm, f32[1]{0:T(128)S(6)} %copy.8.bi_hbm, f32[128,1152]{1,0:T(8,128)} %img_hbm.1, f32[128,1152]{1,0:T(8,128)} %txt_hbm.1), custom_call_target="tpu_custom_call" | custom-call | tf_op jit(solution)/shard_map/pair_loss/pallas_call | solution.py:432
  43.8 2.2 %hand_on.1 = (f32[1,128]{1,0:T(1,128)}, f32[128,1152]{1,0:T(8,128)}, f32[128,1152]{1,0:T(8,128)}) custom-call(f32[1,128]{1,0:T(1,128)} %get-tuple-element.9.row, f32[128,1152]{1,0:T(8,128)} %get-tuple-element.10.gi, f32[128,1152]{1,0:T(8,128)} %get-tuple-element.11.gt), custom_call_target="tpu_custom_call" | custom-call | tf_op jit(solution)/shard_map/hand_on/pallas_call | solution.py:458

commit v5 on v4

--- a/solution.py
+++ b/solution.py
@@ -11,7 +11,7 @@
 MESH = pl.DeviceIdType.MESH
 BF = jnp.bfloat16
 F32 = jnp.float32
-N_SEMS = 44
+N_LANDED = 30
 GROUP = 16
 PARTS = 4
 
@@ -68,20 +68,30 @@
     load_s.start()
     load_b.start()
 
-    sent = []
-
-    def copy_to(src, dst, to):
-        s = len(sent)
+    sent, landed = [], []
+
+    def copy_to(src, dst, to, with_=None):
+        if with_ is None:
+            landed.append(None)
+        slot = len(landed) - 1 if with_ is None else with_[1]
         copy = pltpu.make_async_remote_copy(
-            src_ref=src, dst_ref=dst, send_sem=ssem.at[s], recv_sem=rsem.at[s],
+            src_ref=src, dst_ref=dst, send_sem=ssem.at[0], recv_sem=rsem.at[slot],
             device_id=to, device_id_type=MESH)
         sent.append(copy)
-        return copy
+        return copy, slot
+
+    def start(*copies):
+        for c, _ in copies:
+            c.start()
 
     def arrived(name, *copies):
         with jax.named_scope("wait_" + name):
-            for c in copies:
+            for c, _ in copies:
                 c.wait_recv()
+
+    def all_arrived(name, into, copy):
+        with jax.named_scope("wait_" + name):
+            pltpu.make_async_copy(into, into, rsem.at[copy[1]]).wait()
 
     with jax.named_scope("normalize_text"):
         load_t.wait()
@@ -94,8 +104,7 @@
     t_n = [copy_to(tb.at[OWN0, q], tb.at[NEAR0, q], near_to) for q in quarters]
     t_p1 = copy_to(tb.at[OWN0, h1], tb.at[PAIR0, h1], pair)
     s_own = copy_to(tb.at[OWN0], tb.at[OWN1], sibling)
-    for c in (t_n[3], t_p0, t_n[2], t_p1, t_n[1], t_n[0], s_own):
-        c.start()
+    start(t_n[3], t_p0, t_n[2], t_p1, t_n[1], t_n[0], s_own)
     with jax.named_scope("normalize_image"):
         load_i.wait()
         inv_i = inverse_norm(img[...])
@@ -104,20 +113,21 @@
     i_l1 = copy_to(ib.at[0, h1], ib.at[RIGHT, h1], left)
     i_r1 = copy_to(ib.at[0, h1], ib.at[LEFT, h1], right)
     i_l0 = copy_to(ib.at[0, h0], ib.at[RIGHT, h0], left)
-    for c in (i_r0, i_l1, i_r1, i_l0):
-        c.start()
+    start(i_r0, i_l1, i_r1, i_l0)
     i_o0 = copy_to(ib.at[LEFT, h0], ib.at[OPP, h0], right)
-    i_o1 = copy_to(ib.at[RIGHT, h1], ib.at[OPP, h1], left)
-    s_p0 = copy_to(tb.at[PAIR0, h0], tb.at[PAIR1, h0], sibling)
+    i_o1 = copy_to(ib.at[RIGHT, h1], ib.at[OPP, h1], left, i_o0)
+    s_p0 = copy_to(tb.at[PAIR0, h0], tb.at[PAIR1, h0], sibling, s_own)
     s_n1 = copy_to(tb.at[NEAR0, h1], tb.at[NEAR1, h1], sibling)
-    s_p1 = copy_to(tb.at[PAIR0, h1], tb.at[PAIR1, h1], sibling)
-    s_n0 = copy_to(tb.at[NEAR0, h0], tb.at[NEAR1, h0], sibling)
+    s_p1 = copy_to(tb.at[PAIR0, h1], tb.at[PAIR1, h1], sibling, s_own)
+    s_n0 = copy_to(tb.at[NEAR0, h0], tb.at[NEAR1, h0], sibling, s_n1)
     s_f0 = copy_to(tb.at[FAR0, h0], tb.at[FAR1, h0], sibling)
-    s_f1 = copy_to(tb.at[FAR0, h1], tb.at[FAR1, h1], sibling)
+    s_f1 = copy_to(tb.at[FAR0, h1], tb.at[FAR1, h1], sibling, s_f0)
     t_f0 = copy_to(tb.at[PAIR0, h0], tb.at[FAR0, h0], near_to)
     t_f1 = copy_to(tb.at[NEAR0, h1], tb.at[FAR0, h1], pair)
-    t_q = ([copy_to(tb.at[PAIR0, quarters[0]], tb.at[FAR0, quarters[0]], near_to)]
-           + [copy_to(tb.at[NEAR0, q], tb.at[FAR0, q], pair) for q in quarters[1:]])
+    t_q = [copy_to(tb.at[PAIR0, quarters[0]], tb.at[FAR0, quarters[0]], near_to, t_f0),
+           copy_to(tb.at[NEAR0, quarters[1]], tb.at[FAR0, quarters[1]], pair),
+           copy_to(tb.at[NEAR0, quarters[2]], tb.at[FAR0, quarters[2]], pair),
+           copy_to(tb.at[NEAR0, quarters[3]], tb.at[FAR0, quarters[3]], pair, t_f1)]
     into_first = blk == n_blk - 1
     first = blk == 0
 
@@ -161,18 +171,18 @@
     f_p0 = copy_to(t_out.at[FAR - 1, h0], t_mid.at[0], pair)
     f_n1 = copy_to(t_out.at[FAR - 1, h1], t_mid.at[1], near_of)
     b_p0 = copy_to(t_out.at[PAIR - 1, h0], t_in.at[0, h0], pair)
-    b_p1 = copy_to(t_out.at[PAIR - 1, h1], t_in.at[0, h1], pair)
-    b_n1 = copy_to(t_out.at[NEAR - 1, h1], t_in.at[1, h1], near_of)
-    b_n0 = copy_to(t_out.at[NEAR - 1, h0], t_in.at[1, h0], near_of)
+    b_p1 = copy_to(t_out.at[PAIR - 1, h1], t_in.at[0, h1], pair, b_p0)
+    b_n1 = copy_to(t_out.at[NEAR - 1, h1], t_in.at[1, h1], near_of, b_p0)
+    b_n0 = copy_to(t_out.at[NEAR - 1, h0], t_in.at[1, h0], near_of, b_p0)
     f_r0 = copy_to(i_out.at[OPP - 1, h0], i_mid.at[0], right)
     f_l1 = copy_to(i_out.at[OPP - 1, h1], i_mid.at[1], left)
     b_r1 = copy_to(i_out.at[RIGHT - 1, h1], i_in.at[0, h1], right)
-    b_r0 = copy_to(i_out.at[RIGHT - 1, h0], i_in.at[0, h0], right)
-    b_l0 = copy_to(i_out.at[LEFT - 1, h0], i_in.at[1, h0], left)
-    b_l1 = copy_to(i_out.at[LEFT - 1, h1], i_in.at[1, h1], left)
+    b_r0 = copy_to(i_out.at[RIGHT - 1, h0], i_in.at[0, h0], right, b_r1)
+    b_l0 = copy_to(i_out.at[LEFT - 1, h0], i_in.at[1, h0], left, b_r1)
+    b_l1 = copy_to(i_out.at[LEFT - 1, h1], i_in.at[1, h1], left, b_r1)
     l_o = copy_to(loss.at[OPP], l_mid, right)
     l_r = copy_to(loss.at[RIGHT], l_in.at[0], right)
-    l_l = copy_to(loss.at[LEFT], l_in.at[1], left)
+    l_l = copy_to(loss.at[LEFT], l_in.at[1], left, l_r)
 
     def text_partial(first, last):
         return jnp.dot(coef[first * rows:last * rows], ib[...].reshape(4 * rows, width),
@@ -180,7 +190,7 @@
 
     def to_sibling(s, part):
         sib_out[s] = part.astype(BF)
-        back[s].start()
+        start(back[s])
 
     def add_sibling(s, part):
         arrived(f"text_sibling_{s}", back[s])
@@ -189,12 +199,12 @@
     def pass_on(name, got, src, slot, part, middle, out):
         arrived(name, got)
         src[slot, part] = (src[slot, part].astype(F32) + middle[...].astype(F32)).astype(BF)
-        out.start()
+        start(out)
 
     def pass_loss():
         arrived("mid_loss", l_o)
         loss[RIGHT] += l_mid[...]
-        l_r.start()
+        start(l_r)
 
     def pass_right():
         pass_on("mid_r", f_r0, i_out, RIGHT - 1, h0, i_mid.at[0], b_r0)
@@ -208,6 +218,7 @@
     def pass_pair():
         pass_on("mid_p", f_n1, t_out, PAIR - 1, h1, t_mid.at[1], b_p1)
 
+    assert len(landed) == N_LANDED
     puts = [pltpu.make_async_copy(held, out, lsem.at[i])
             for i, (held, out) in enumerate(((row, loss_hbm), (gi, gi_hbm), (gt, gt_hbm)))]
 
@@ -216,20 +227,20 @@
         return inverse * (grad - unit * jnp.sum(unit * grad, axis=1, keepdims=True))
 
     def finish_loss():
-        arrived("loss", l_r, l_l)
+        all_arrived("loss", l_in, l_r)
         total = loss[0] + l_in[0] + l_in[1]
         row[...] = jnp.sum(total, axis=0, keepdims=True) / mean
         puts[0].start()
 
     def finish_image():
-        arrived("image_back", b_r1, b_l0, b_r0, b_l1)
+        all_arrived("image_back", i_in, b_r1)
         with jax.named_scope("image_norm"):
             grad = gi[...] + i_in[0].astype(F32) + i_in[1].astype(F32)
             gi[...] = backnorm(img[...], inv_i, grad)
             puts[1].start()
 
     def finish_text():
-        arrived("text_back", b_p0, b_n1, b_n0, b_p1)
+        all_arrived("text_back", t_in, b_p0)
         with jax.named_scope("text_norm"):
             grad = gt[...] + t_in[0].astype(F32) + t_in[1].astype(F32)
             gt[...] = backnorm(txt[...], inv_t, grad)
@@ -237,50 +248,50 @@
 
     def start_own_plane():
         arrived("first_p", t_p0)
-        pl.when(into_first)(t_q[0].start)
-        pl.when(jnp.logical_not(into_first))(t_f0.start)
-        s_p0.start()
+        pl.when(into_first)(t_q[0][0].start)
+        pl.when(jnp.logical_not(into_first))(t_f0[0].start)
+        start(s_p0)
         arrived("first_i", i_r0, i_l1)
-        i_o0.start()
-        i_o1.start()
+        start(i_o0)
+        start(i_o1)
 
     @pl.when(jnp.logical_not(first))
     def _():
         start_own_plane()
         arrived("first_n", t_n[3], t_n[2])
-        t_f1.start()
-        s_n1.start()
+        start(t_f1)
+        start(s_n1)
         arrived("second_p", t_p1)
-        s_p1.start()
+        start(s_p1)
         arrived("second_n", t_n[1], t_n[0])
-        s_n0.start()
+        start(s_n0)
         arrived("second_i", i_r1, i_l0)
         score(OWN0, OWN1, 0, OPP)
-        arrived("pair_sibling", s_own, s_p0, s_p1)
+        all_arrived("pair_sibling", tb.at[OWN1:NEAR0], s_own)
         score(OWN1, NEAR0, 0, OPP)
-        arrived("near_sibling", s_n1, s_n0)
+        all_arrived("near_sibling", tb.at[NEAR1], s_n1)
         score(NEAR0, FAR0, 0, OPP)
         arrived("far_t0", t_f0)
-        s_f0.start()
+        start(s_f0)
         arrived("far_t1", t_f1)
-        s_f1.start()
-        arrived("opp_i", i_o0, i_o1)
+        start(s_f1)
+        all_arrived("opp_i", ib.at[OPP], i_o0)
         score(OWN0, FAR0, OPP, OPP + 1)
         score(FAR0, FAR1, 0, OPP + 1)
-        arrived("far_sibling", s_f0, s_f1)
+        all_arrived("far_sibling", tb.at[FAR1], s_f0)
         score(FAR1, FAR1 + 1, 0, OPP + 1)
-        l_o.start()
-        l_l.start()
+        start(l_o)
+        start(l_l)
         with jax.named_scope("text_far_1"):
             to_sibling(FAR, text_partial(FAR1, FAR1 + 1))
         with jax.named_scope("image_opp"):
             i_out[OPP - 1] = image_partial(OPP, OPP + 1, OWN0, FAR1 + 1).astype(BF)
-            f_r0.start()
-            f_l1.start()
+            start(f_r0)
+            start(f_l1)
         with jax.named_scope("text_far_0"):
             t_out[FAR - 1] = add_sibling(FAR, text_partial(FAR0, FAR1)).astype(BF)
-            f_p0.start()
-            f_n1.start()
+            start(f_p0)
+            start(f_n1)
         with jax.named_scope("text_mid"):
             mid = text_partial(OWN1, FAR0)
             to_sibling(PAIR, mid[rows:2 * rows])
@@ -290,15 +301,15 @@
         with jax.named_scope("image_next"):
             part = image_partial(RIGHT, LEFT + 1, OWN0, FAR1 + 1)
             i_out[RIGHT - 1:LEFT] = part.astype(BF).reshape(2, rows, width)
-            b_r1.start()
-            b_l0.start()
+            start(b_r1)
+            start(b_l0)
         with jax.named_scope("text_near"):
             t_out[NEAR - 1] = add_sibling(NEAR, near).astype(BF)
-            b_n1.start()
+            start(b_n1)
         with jax.named_scope("text_own"):
             own = text_partial(OWN0, OWN1)
             t_out[PAIR - 1] = add_sibling(PAIR, own[rows:]).astype(BF)
-            b_p0.start()
+            start(b_p0)
             gt[...] = own[:rows]
         with jax.named_scope("image_own"):
             gi[...] = image_partial(0, 1, OWN0, FAR1 + 1)
@@ -316,20 +327,20 @@
     def _():
         start_own_plane()
         arrived("second_p", t_p1)
-        s_p1.start()
+        start(s_p1)
         arrived("second_i", i_r1, i_l0)
         score(OWN0, OWN1, 0, OPP)
-        arrived("pair_sibling", s_own, s_p0, s_p1)
+        all_arrived("pair_sibling", tb.at[OWN1:NEAR0], s_own)
         score(OWN1, NEAR0, 0, OPP)
-        arrived("opp_i", i_o0, i_o1)
+        all_arrived("opp_i", ib.at[OPP], i_o0)
         score(OWN0, NEAR0, OPP, OPP + 1)
         arrived("first_n", t_n[3])
-        t_q[3].start()
+        start(t_q[3])
         arrived("second_n", t_n[2])
-        t_q[2].start()
-        s_n1.start()
+        start(t_q[2])
+        start(s_n1)
         arrived("third_n", t_n[1])
-        t_q[1].start()
+        start(t_q[1])
         with jax.named_scope("text_block"):
             part = text_partial(OWN0, NEAR0)
             to_sibling(PAIR, part[3 * rows:])
@@ -337,27 +348,28 @@
             gt[...] = part[:rows]
             kept[...] = part[rows:2 * rows]
         arrived("last_n", t_n[0])
-        s_n0.start()
+        start(s_n0)
         score(NEAR0, NEAR1, 0, OPP + 1)
-        arrived("near_sibling", s_n1, s_n0)
+        all_arrived("near_sibling", tb.at[NEAR1], s_n1)
         score(NEAR1, FAR0, 0, OPP + 1)
         arrived("far_t1", t_q[3], t_q[2])
-        s_f1.start()
+        start(s_f1)
         arrived("far_t0", t_q[0], t_q[1])
-        s_f0.start()
+        start(s_f0)
         score(FAR0, FAR1, 0, OPP + 1)
         with jax.named_scope("image_ahead"):
             gi[...] = image_partial(OPP, OPP + 1, OWN0, FAR0)
         t_out[PAIR - 1] = add_sibling(PAIR, kept[...]).astype(BF)
-        b_p0.start()
-        arrived("far_sibling", s_f0, s_f1)
-        score(FAR1, FAR1 + 1, 0, OPP + 1)
-        l_o.start()
-        l_l.start()
+        start(b_p0)
+        all_arrived("far_sibling", tb.at[FAR1], s_f0)
+        score(FAR1, FAR1 + 1, OPP, OPP + 1)
         with jax.named_scope("image_opp"):
             i_out[OPP - 1] = (gi[...] + image_partial(OPP, OPP + 1, FAR0, FAR1 + 1)).astype(BF)
-            f_r0.start()
-            f_l1.start()
+            start(f_r0)
+            start(f_l1)
+        score(FAR1, FAR1 + 1, 0, OPP)
+        start(l_o)
+        start(l_l)
         with jax.named_scope("text_far"):
             part = text_partial(NEAR0, FAR1 + 1)
             to_sibling(FAR, part[3 * rows:])
@@ -367,13 +379,13 @@
         with jax.named_scope("image_next"):
             part = image_partial(RIGHT, OPP, OWN0, FAR1 + 1)
             i_out[RIGHT - 1:LEFT] = part.astype(BF).reshape(2, rows, width)
-            b_r1.start()
-            b_l0.start()
+            start(b_r1)
+            start(b_l0)
         t_out[FAR - 1] = add_sibling(FAR, kept[...]).astype(BF)
-        f_p0.start()
-        f_n1.start()
+        start(f_p0)
+        start(f_n1)
         t_out[NEAR - 1] = add_sibling(NEAR, near).astype(BF)
-        b_n1.start()
+        start(b_n1)
         pass_pair()
         gt[...] = add_sibling(OWN, gt[...])
         with jax.named_scope("image_own"):
@@ -387,13 +399,14 @@
         finish_image()
 
     with jax.named_scope("sends_end"):
+        some = [t_f0[0], t_f1[0]] + [c for c, _ in t_q]
         for c in sent:
-            if not any(c is o for o in (t_f0, t_f1, *t_q)):
+            if not any(c is o for o in some):
                 c.wait_send()
-        pl.when(into_first)(t_q[0].wait_send)
-        pl.when(jnp.logical_not(into_first))(t_f0.wait_send)
-        pl.when(jnp.logical_not(first))(t_f1.wait_send)
-        for c in t_q[1:]:
+        pl.when(into_first)(t_q[0][0].wait_send)
+        pl.when(jnp.logical_not(into_first))(t_f0[0].wait_send)
+        pl.when(jnp.logical_not(first))(t_f1[0].wait_send)
+        for c, _ in t_q[1:]:
             pl.when(first)(c.wait_send)
     with jax.named_scope("put"):
         for c in puts:
@@ -448,8 +461,8 @@
             low((3, rows, width)), low((2, rows // 2, width)), low((2, rows, width)),
             full((8, rows)), full((2, 8, rows)),
             pltpu.SemaphoreType.DMA((4,)),
-            pltpu.SemaphoreType.DMA((N_SEMS,)),
-            pltpu.SemaphoreType.DMA((N_SEMS,)),
+            pltpu.SemaphoreType.DMA((1,)),
+            pltpu.SemaphoreType.DMA((N_LANDED,)),
         ],
         compiler_params=pltpu.CompilerParams(
             collective_id=0, has_side_effects=True, vmem_limit_bytes=(64 << 20) - (1 << 19)),

time: 46.3 us -> 46 us (level)
  no operation moved by 1% of the time
where the time goes in v5:
time: 46 us; the launch traced here: 45.8 us
  Pallas kernels  43.7 us (95%)
  between operations  2.09 us (5%)
    pallas_call x1, Pallas kernels, body(): pl.pallas_call(functools.partial(kernel, n_blk, mean), out_shape=results,...  41.5 us
    pallas_call x1, Pallas kernels, body(): pl.pallas_call(hand_on, out_shape=results, in_specs=[anywhere] * 3, out_s...  2.17 us

profile of v5, /device:TPU:1, one launch (start us, length us, event | category | flops | bytes accessed | tf_op | source)
XLA Modules:
  0.0 45.8 jit_solution(6432949801760486075)
XLA Ops:
  1.9 41.5 %pair_loss.1 = (f32[1,128]{1,0:T(1,128)}, f32[128,1152]{1,0:T(8,128)}, f32[128,1152]{1,0:T(8,128)}) custom-call(f32[1]{0:T(128)S(6)} %copy.7.ls_hbm, f32[1]{0:T(128)S(6)} %copy.8.bi_hbm, f32[128,1152]{1,0:T(8,128)} %img_hbm.1, f32[128,1152]{1,0:T(8,128)} %txt_hbm.1), custom_call_target="tpu_custom_call" | custom-call | tf_op jit(solution)/shard_map/pair_loss/pallas_call | solution.py:445
  43.5 2.2 %hand_on.1 = (f32[1,128]{1,0:T(1,128)}, f32[128,1152]{1,0:T(8,128)}, f32[128,1152]{1,0:T(8,128)}) custom-call(f32[1,128]{1,0:T(1,128)} %get-tuple-element.9.row, f32[128,1152]{1,0:T(8,128)} %get-tuple-element.10.gi, f32[128,1152]{1,0:T(8,128)} %get-tuple-element.11.gt), custom_call_target="tpu_custom_call" | custom-call | tf_op jit(solution)/shard_map/hand_on/pallas_call | solution.py:471

commit v6 on v5

--- a/solution.py
+++ b/solution.py
@@ -220,7 +220,8 @@
 
     assert len(landed) == N_LANDED
     puts = [pltpu.make_async_copy(held, out, lsem.at[i])
-            for i, (held, out) in enumerate(((row, loss_hbm), (gi, gi_hbm), (gt, gt_hbm)))]
+            for i, (held, out) in enumerate(((row, loss_hbm), (gt, gt_hbm), (gi.at[h0], gi_hbm.at[h0]),
+                                             (gi.at[h1], gi_hbm.at[h1])))]
 
     def backnorm(values, inverse, grad):
         unit = values * inverse
@@ -235,16 +236,18 @@
     def finish_image():
         all_arrived("image_back", i_in, b_r1)
         with jax.named_scope("image_norm"):
-            grad = gi[...] + i_in[0].astype(F32) + i_in[1].astype(F32)
-            gi[...] = backnorm(img[...], inv_i, grad)
-            puts[1].start()
+            for at, put in ((0, puts[2]), (half, puts[3])):
+                part = pl.ds(at, half)
+                grad = gi[part] + i_in[0, part].astype(F32) + i_in[1, part].astype(F32)
+                gi[part] = backnorm(img[part], inv_i[at:at + half], grad)
+                put.start()
 
     def finish_text():
         all_arrived("text_back", t_in, b_p0)
         with jax.named_scope("text_norm"):
             grad = gt[...] + t_in[0].astype(F32) + t_in[1].astype(F32)
             gt[...] = backnorm(txt[...], inv_t, grad)
-            puts[2].start()
+            puts[1].start()
 
     def start_own_plane():
         arrived("first_p", t_p0)
@@ -337,16 +340,15 @@
         arrived("first_n", t_n[3])
         start(t_q[3])
         arrived("second_n", t_n[2])
-        start(t_q[2])
-        start(s_n1)
-        arrived("third_n", t_n[1])
-        start(t_q[1])
+        start(t_q[2], s_n1)
         with jax.named_scope("text_block"):
             part = text_partial(OWN0, NEAR0)
             to_sibling(PAIR, part[3 * rows:])
             to_sibling(OWN, part[2 * rows:3 * rows])
             gt[...] = part[:rows]
             kept[...] = part[rows:2 * rows]
+        arrived("third_n", t_n[1])
+        start(t_q[1])
         arrived("last_n", t_n[0])
         start(s_n0)
         score(NEAR0, NEAR1, 0, OPP + 1)
@@ -359,35 +361,31 @@
         score(FAR0, FAR1, 0, OPP + 1)
         with jax.named_scope("image_ahead"):
             gi[...] = image_partial(OPP, OPP + 1, OWN0, FAR0)
-        t_out[PAIR - 1] = add_sibling(PAIR, kept[...]).astype(BF)
-        start(b_p0)
         all_arrived("far_sibling", tb.at[FAR1], s_f0)
         score(FAR1, FAR1 + 1, OPP, OPP + 1)
         with jax.named_scope("image_opp"):
             i_out[OPP - 1] = (gi[...] + image_partial(OPP, OPP + 1, FAR0, FAR1 + 1)).astype(BF)
-            start(f_r0)
-            start(f_l1)
+            start(f_r0, f_l1)
+        t_out[PAIR - 1] = add_sibling(PAIR, kept[...]).astype(BF)
+        start(b_p0)
         score(FAR1, FAR1 + 1, 0, OPP)
-        start(l_o)
-        start(l_l)
-        with jax.named_scope("text_far"):
-            part = text_partial(NEAR0, FAR1 + 1)
-            to_sibling(FAR, part[3 * rows:])
-            to_sibling(NEAR, part[rows:2 * rows])
-            kept[...] = part[2 * rows:3 * rows]
-            near = part[:rows]
+        start(l_o, l_l)
+        with jax.named_scope("text_far_1"):
+            to_sibling(FAR, text_partial(FAR1, FAR1 + 1))
         with jax.named_scope("image_next"):
             part = image_partial(RIGHT, OPP, OWN0, FAR1 + 1)
             i_out[RIGHT - 1:LEFT] = part.astype(BF).reshape(2, rows, width)
-            start(b_r1)
-            start(b_l0)
-        t_out[FAR - 1] = add_sibling(FAR, kept[...]).astype(BF)
-        start(f_p0)
-        start(f_n1)
-        t_out[NEAR - 1] = add_sibling(NEAR, near).astype(BF)
-        start(b_n1)
+            start(b_r1, b_l0)
+        with jax.named_scope("text_far_0"):
+            t_out[FAR - 1] = add_sibling(FAR, text_partial(FAR0, FAR1)).astype(BF)
+            start(f_p0, f_n1)
+        with jax.named_scope("text_near"):
+            near = text_partial(NEAR0, FAR0)
+            to_sibling(NEAR, near[rows:])
         pass_pair()
         gt[...] = add_sibling(OWN, gt[...])
+        t_out[NEAR - 1] = add_sibling(NEAR, near[:rows]).astype(BF)
+        start(b_n1)
         with jax.named_scope("image_own"):
             gi[...] = image_partial(0, 1, OWN0, FAR1 + 1)
         pass_loss()

time: 46 us -> 45.4 us (0.987)
  Pallas kernels: 43.7 us -> 43.1 us
    pallas_call x1, Pallas kernels: 41.5 us -> 40.9 us  [body(): pl.pallas_call(functools.partial(kernel, n_blk, mean), out_shape=results,...]
where the time goes in v6:
time: 45.4 us; the launch traced here: 45.2 us
  Pallas kernels  43.1 us (95%)
  between operations  2.09 us (5%)
    pallas_call x1, Pallas kernels, body(): pl.pallas_call(functools.partial(kernel, n_blk, mean), out_shape=results,...  40.9 us
    pallas_call x1, Pallas kernels, body(): pl.pallas_call(hand_on, out_shape=results, in_specs=[anywhere] * 3, out_s...  2.17 us

profile of v6, /device:TPU:1, one launch (start us, length us, event | category | flops | bytes accessed | tf_op | source)
XLA Modules:
  0.0 45.2 jit_solution(3846074710701533427)
XLA Ops:
  1.9 40.9 %pair_loss.1 = (f32[1,128]{1,0:T(1,128)}, f32[128,1152]{1,0:T(8,128)}, f32[128,1152]{1,0:T(8,128)}) custom-call(f32[1]{0:T(128)S(6)} %copy.7.ls_hbm, f32[1]{0:T(128)S(6)} %copy.8.bi_hbm, f32[128,1152]{1,0:T(8,128)} %img_hbm.1, f32[128,1152]{1,0:T(8,128)} %txt_hbm.1), custom_call_target="tpu_custom_call" | custom-call | tf_op jit(solution)/shard_map/pair_loss/pallas_call | solution.py:443
  42.8 2.2 %hand_on.1 = (f32[1,128]{1,0:T(1,128)}, f32[128,1152]{1,0:T(8,128)}, f32[128,1152]{1,0:T(8,128)}) custom-call(f32[1,128]{1,0:T(1,128)} %get-tuple-element.9.row, f32[128,1152]{1,0:T(8,128)} %get-tuple-element.10.gi, f32[128,1152]{1,0:T(8,128)} %get-tuple-element.11.gt), custom_call_target="tpu_custom_call" | custom-call | tf_op jit(solution)/shard_map/hand_on/pallas_call | solution.py:469

commit v7 on v6

--- a/solution.py
+++ b/solution.py
@@ -144,13 +144,14 @@
                                    (((1,), (1,)), ((), ())), preferred_element_type=F32)
             logit = temper * dots + offset
             e = jnp.exp(-jnp.abs(logit))
-            weight = jnp.where(logit >= 0, 1.0, e) * pl.reciprocal(1.0 + e, approx=True)
-            signed = logit
+            signed, paired = logit, None
             if first == OWN0 and lo == 0:
                 r = lax.broadcasted_iota(jnp.int32, logit.shape, 0)
                 paired = (r == lax.broadcasted_iota(jnp.int32, logit.shape, 1)) & (r < rows)
-                weight = weight - paired.astype(F32)
                 signed = jnp.where(paired, -logit, logit)
+            weight = jnp.where(signed >= 0, 1.0, e) * pl.reciprocal(1.0 + e, approx=True)
+            if paired is not None:
+                weight = jnp.where(paired, -weight, weight)
             coef[pl.ds(first * rows, n), pl.ds(lo * rows, m)] = (temper * weight).astype(BF)
             e = e.reshape(n // (8 * GROUP), GROUP, 8, m)
             p = e[:, 0]

time: 45.4 us -> 45.4 us (level)
  no operation moved by 1% of the time
where the time goes in v7:
time: 45.4 us; the launch traced here: 45.2 us
  Pallas kernels  43.1 us (95%)
  between operations  2.09 us (5%)
    pallas_call x1, Pallas kernels, body(): pl.pallas_call(functools.partial(kernel, n_blk, mean), out_shape=results,...  40.9 us
    pallas_call x1, Pallas kernels, body(): pl.pallas_call(hand_on, out_shape=results, in_specs=[anywhere] * 3, out_s...  2.17 us

profile of v7, /device:TPU:1, one launch (start us, length us, event | category | flops | bytes accessed | tf_op | source)
XLA Modules:
  0.0 45.2 jit_solution(2992739463862117412)
XLA Ops:
  1.9 40.9 %pair_loss.1 = (f32[1,128]{1,0:T(1,128)}, f32[128,1152]{1,0:T(8,128)}, f32[128,1152]{1,0:T(8,128)}) custom-call(f32[1]{0:T(128)S(6)} %copy.7.ls_hbm, f32[1]{0:T(128)S(6)} %copy.8.bi_hbm, f32[128,1152]{1,0:T(8,128)} %img_hbm.1, f32[128,1152]{1,0:T(8,128)} %txt_hbm.1), custom_call_target="tpu_custom_call" | custom-call | tf_op jit(solution)/shard_map/pair_loss/pallas_call | solution.py:444
  42.8 2.2 %hand_on.1 = (f32[1,128]{1,0:T(1,128)}, f32[128,1152]{1,0:T(8,128)}, f32[128,1152]{1,0:T(8,128)}) custom-call(f32[1,128]{1,0:T(1,128)} %get-tuple-element.9.row, f32[128,1152]{1,0:T(8,128)} %get-tuple-element.10.gi, f32[128,1152]{1,0:T(8,128)} %get-tuple-element.11.gt), custom_call_target="tpu_custom_call" | custom-call | tf_op jit(solution)/shard_map/hand_on/pallas_call | solution.py:470

commit v8 on v7

--- a/solution.py
+++ b/solution.py
@@ -137,7 +137,7 @@
     offset = bi_ref[0]
     loss[...] = jnp.zeros_like(loss)
 
-    def score(first, last, lo, hi):
+    def score(first, last, lo, hi, weights=True, losses=True):
         with jax.named_scope(f"score_{first}_{last}_{lo}_{hi}"):
             n, m = (last - first) * rows, (hi - lo) * rows
             dots = lax.dot_general(tb[first:last].reshape(n, width), ib[lo:hi].reshape(m, width),
@@ -149,10 +149,13 @@
                 r = lax.broadcasted_iota(jnp.int32, logit.shape, 0)
                 paired = (r == lax.broadcasted_iota(jnp.int32, logit.shape, 1)) & (r < rows)
                 signed = jnp.where(paired, -logit, logit)
-            weight = jnp.where(signed >= 0, 1.0, e) * pl.reciprocal(1.0 + e, approx=True)
-            if paired is not None:
-                weight = jnp.where(paired, -weight, weight)
-            coef[pl.ds(first * rows, n), pl.ds(lo * rows, m)] = (temper * weight).astype(BF)
+            if weights:
+                weight = jnp.where(signed >= 0, 1.0, e) * pl.reciprocal(1.0 + e, approx=True)
+                if paired is not None:
+                    weight = jnp.where(paired, -weight, weight)
+                coef[pl.ds(first * rows, n), pl.ds(lo * rows, m)] = (temper * weight).astype(BF)
+            if not losses:
+                return
             e = e.reshape(n // (8 * GROUP), GROUP, 8, m)
             p = e[:, 0]
             for g in range(1, GROUP):
@@ -363,13 +366,14 @@
         with jax.named_scope("image_ahead"):
             gi[...] = image_partial(OPP, OPP + 1, OWN0, FAR0)
         all_arrived("far_sibling", tb.at[FAR1], s_f0)
-        score(FAR1, FAR1 + 1, OPP, OPP + 1)
+        score(FAR1, FAR1 + 1, OPP, OPP + 1, losses=False)
         with jax.named_scope("image_opp"):
             i_out[OPP - 1] = (gi[...] + image_partial(OPP, OPP + 1, FAR0, FAR1 + 1)).astype(BF)
             start(f_r0, f_l1)
         t_out[PAIR - 1] = add_sibling(PAIR, kept[...]).astype(BF)
         start(b_p0)
         score(FAR1, FAR1 + 1, 0, OPP)
+        score(FAR1, FAR1 + 1, OPP, OPP + 1, weights=False)
         start(l_o, l_l)
         with jax.named_scope("text_far_1"):
             to_sibling(FAR, text_partial(FAR1, FAR1 + 1))

time: 45.4 us -> 45.4 us (level)
  no operation moved by 1% of the time
where the time goes in v8:
time: 45.4 us; the launch traced here: 45.2 us
  Pallas kernels  43.1 us (95%)
  between operations  2.09 us (5%)
    pallas_call x1, Pallas kernels, body(): pl.pallas_call(functools.partial(kernel, n_blk, mean), out_shape=results,...  40.9 us
    pallas_call x1, Pallas kernels, body(): pl.pallas_call(hand_on, out_shape=results, in_specs=[anywhere] * 3, out_s...  2.17 us

profile of v8, /device:TPU:1, one launch (start us, length us, event | category | flops | bytes accessed | tf_op | source)
XLA Modules:
  0.0 45.2 jit_solution(4870812065621493917)
XLA Ops:
  1.9 40.9 %pair_loss.1 = (f32[1,128]{1,0:T(1,128)}, f32[128,1152]{1,0:T(8,128)}, f32[128,1152]{1,0:T(8,128)}) custom-call(f32[1]{0:T(128)S(6)} %copy.7.ls_hbm, f32[1]{0:T(128)S(6)} %copy.8.bi_hbm, f32[128,1152]{1,0:T(8,128)} %img_hbm.1, f32[128,1152]{1,0:T(8,128)} %txt_hbm.1), custom_call_target="tpu_custom_call" | custom-call | tf_op jit(solution)/shard_map/pair_loss/pallas_call | solution.py:448
  42.8 2.2 %hand_on.1 = (f32[1,128]{1,0:T(1,128)}, f32[128,1152]{1,0:T(8,128)}, f32[128,1152]{1,0:T(8,128)}) custom-call(f32[1,128]{1,0:T(1,128)} %get-tuple-element.9.row, f32[128,1152]{1,0:T(8,128)} %get-tuple-element.10.gi, f32[128,1152]{1,0:T(8,128)} %get-tuple-element.11.gt), custom_call_target="tpu_custom_call" | custom-call | tf_op jit(solution)/shard_map/hand_on/pallas_call | solution.py:474

commit v9 on v7

--- a/solution.py
+++ b/solution.py
@@ -13,7 +13,7 @@
 F32 = jnp.float32
 N_LANDED = 30
 GROUP = 16
-PARTS = 4
+PARTS = 2
 
 OWN0, PAIR0, OWN1, PAIR1, NEAR0, NEAR1, FAR0, FAR1 = range(8)
 OWN, PAIR, NEAR, FAR = range(4)

time: 45.4 us -> 45.2 us (level)
  no operation moved by 1% of the time
where the time goes in v9:
time: 45.2 us; the launch traced here: 45.1 us
  Pallas kernels  43 us (95%)
  between operations  2.09 us (5%)
    pallas_call x1, Pallas kernels, body(): pl.pallas_call(functools.partial(kernel, n_blk, mean), out_shape=results,...  40.9 us
    pallas_call x1, Pallas kernels, body(): pl.pallas_call(hand_on, out_shape=results, in_specs=[anywhere] * 3, out_s...  2.06 us

profile of v9, /device:TPU:1, one launch (start us, length us, event | category | flops | bytes accessed | tf_op | source)
XLA Modules:
  0.0 45.1 jit_solution(11726153189905353842)
XLA Ops:
  1.9 40.9 %pair_loss.1 = (f32[1,128]{1,0:T(1,128)}, f32[128,1152]{1,0:T(8,128)}, f32[128,1152]{1,0:T(8,128)}) custom-call(f32[1]{0:T(128)S(6)} %copy.7.ls_hbm, f32[1]{0:T(128)S(6)} %copy.8.bi_hbm, f32[128,1152]{1,0:T(8,128)} %img_hbm.1, f32[128,1152]{1,0:T(8,128)} %txt_hbm.1), custom_call_target="tpu_custom_call" | custom-call | tf_op jit(solution)/shard_map/pair_loss/pallas_call | solution.py:444
  42.8 2.1 %hand_on.1 = (f32[1,128]{1,0:T(1,128)}, f32[128,1152]{1,0:T(8,128)}, f32[128,1152]{1,0:T(8,128)}) custom-call(f32[1,128]{1,0:T(1,128)} %get-tuple-element.9.row, f32[128,1152]{1,0:T(8,128)} %get-tuple-element.10.gi, f32[128,1152]{1,0:T(8,128)} %get-tuple-element.11.gt), custom_call_target="tpu_custom_call" | custom-call | tf_op jit(solution)/shard_map/hand_on/pallas_call | solution.py:470
